TPU v7x, 32 devices: a whole 2x2x4 slice. The times are simulated.
32 devices in a mesh: ctx: 4 (over x, core), head: 8 (over z, y).
Axes of the slice: x: 2, y: 2, z: 4, core: 2. Of those that a mesh axis runs over, the one named last changes fastest.
Arguments:
- queries: bfloat16 [8192, 8192], P(('ctx', 'head')), may hold values from -30 to 30
- keys: bfloat16 [8192, 8192], P(('ctx', 'head')), may hold values from -30 to 30
- values: bfloat16 [8192, 8192], P(('ctx', 'head')), may hold values from -6 to 6
- rates: bfloat16 [8192, 32], P(('ctx', 'head')), may hold values from 0.0009994507 to 0.0099487305
- fast_init: bfloat16 [3, 32, 256, 256], P(None, 'head'), may hold values from -0.375 to 0.375
- gain: float32 [8192], replicated, may hold values from 0.25 to 1.75
Outputs:
- mixed: bfloat16 [8192, 8192], P(('ctx', 'head'))
All inputs are finite; a program needn't handle non-finite values.
Results may differ from a plain program's by a relative error of at most 0.0095.
Values may be sent and summed in bfloat16 or wider, within the bound.
No kernel may reach another device: no remote copies, remote signals or barrier semaphores. Data moves between devices by JAX's collectives and lax.ppermute only.
A program may use at most 192 MiB of HBM per device.

v0:
```python
import jax
import jax.numpy as jnp
from jax import lax
from jax.sharding import PartitionSpec as P

WINDOW = 2048


EPSILON = 1e-06


def from_behind(value, axis, steps):
    count = lax.axis_size(axis)
    initial, last = (max(0, -steps), min(count, count - steps))
    return lax.ppermute(value, axis, [(source, source + steps) for source in range(initial, last)])


def silu_parts(pre):
    sigma = jax.nn.sigmoid(pre)
    return (pre * sigma, sigma)


def on_device(queries, keys, values, rates, fast_init, gain):
    q_rows, k_rows, v_rows, rate_rows = (
        lax.all_to_all(queries, "head", split_axis=1, concat_axis=0, tiled=True),
        lax.all_to_all(keys, "head", split_axis=1, concat_axis=0, tiled=True),
        lax.all_to_all(values, "head", split_axis=1, concat_axis=0, tiled=True),
        lax.all_to_all(rates, "head", split_axis=1, concat_axis=0, tiled=True),
    )
    length = q_rows.shape[0]
    heads_here = fast_init.shape[1]
    head_size = fast_init.shape[3]
    columns = heads_here * head_size
    query_heads = q_rows.reshape(length, heads_here, head_size)
    key_heads = k_rows.reshape(length, heads_here, head_size)
    value_heads = v_rows.reshape(length, heads_here, head_size)
    edge_keys, edge_values = from_behind((k_rows, v_rows), "ctx", 1)
    key_ext = jnp.concatenate([edge_keys, k_rows], 0).reshape(
        WINDOW + length, heads_here, head_size
    )
    value_ext = jnp.concatenate([edge_values, v_rows], 0).reshape(
        WINDOW + length, heads_here, head_size
    )
    anchor = lax.axis_index("ctx") * length
    block = min(512, length)
    scale = head_size ** (-0.5)

    def attend(number):
        start = number * block
        query_block = lax.dynamic_slice_in_dim(query_heads, start, block, 0)
        key_block = lax.dynamic_slice_in_dim(key_ext, start, block + WINDOW, 0)
        value_block = lax.dynamic_slice_in_dim(value_ext, start, block + WINDOW, 0)
        scores = (
            jnp.einsum("qhd,khd->hqk", query_block, key_block, preferred_element_type=jnp.float32)
            * scale
        )
        query_pos = anchor + start + jnp.arange(block, dtype=jnp.int32)[:, None]
        key_pos = anchor + start - WINDOW + jnp.arange(block + WINDOW, dtype=jnp.int32)[None, :]
        valid = ((key_pos <= query_pos) & (key_pos > query_pos - WINDOW) & (key_pos >= 0))[None]
        masked = jnp.where(valid, scores, -jnp.inf)
        top = jnp.max(masked, axis=2, keepdims=True)
        weights = jnp.where(valid, jnp.exp(masked - top), 0.0)
        probs = (weights / jnp.sum(weights, axis=2, keepdims=True)).astype(jnp.bfloat16)
        return jnp.einsum("hqk,khd->qhd", probs, value_block, preferred_element_type=jnp.float32)

    attended = lax.map(attend, jnp.arange(length // block, dtype=jnp.int32)).reshape(
        length, columns
    )
    targets = (rate_rows.astype(jnp.float32)[:, :, None] * value_heads.astype(jnp.float32)).astype(
        jnp.bfloat16
    )
    gate_pre = jnp.einsum(
        "thd,hfd->thf", key_heads, fast_init[0], preferred_element_type=jnp.float32
    )
    up_pre = jnp.einsum("thd,hfd->thf", key_heads, fast_init[1], preferred_element_type=jnp.float32)
    gate_act, sigma = silu_parts(gate_pre)
    hidden = (gate_act * up_pre).astype(jnp.bfloat16)
    back = jnp.einsum("thd,hfd->thf", targets, fast_init[2], preferred_element_type=jnp.float32)
    back_gate = (back * up_pre * sigma * (1.0 + gate_pre * (1.0 - sigma))).astype(jnp.bfloat16)
    back_up = (back * gate_act).astype(jnp.bfloat16)
    totals = jnp.stack(
        [
            jnp.einsum("thf,thd->hfd", back_gate, key_heads, preferred_element_type=jnp.float32),
            jnp.einsum("thf,thd->hfd", back_up, key_heads, preferred_element_type=jnp.float32),
            jnp.einsum("thf,thd->hfd", hidden, targets, preferred_element_type=jnp.float32),
        ]
    )
    own_index = lax.axis_index("ctx")
    piece = lax.all_gather(totals[None], "ctx", axis=0, tiled=True)
    owners = jnp.arange(piece.shape[0], dtype=jnp.int32)
    keep = (owners < own_index).astype(jnp.float32)
    earlier = jnp.sum(piece * keep[:, None, None, None, None], axis=0)
    initial = fast_init.astype(jnp.float32)
    target_ms = jnp.mean(initial * initial, axis=3, keepdims=True)
    renewed = initial + earlier
    current = jnp.mean(renewed * renewed, axis=3, keepdims=True)
    fitted = (renewed * jnp.sqrt(target_ms) * lax.rsqrt(current + EPSILON)).astype(jnp.bfloat16)
    q_gate = jnp.einsum("thd,hfd->thf", query_heads, fitted[0], preferred_element_type=jnp.float32)
    q_up = jnp.einsum("thd,hfd->thf", query_heads, fitted[1], preferred_element_type=jnp.float32)
    q_hidden = (silu_parts(q_gate)[0] * q_up).astype(jnp.bfloat16)
    recalled = jnp.einsum("thf,hfd->thd", q_hidden, fitted[2], preferred_element_type=jnp.float32)
    combined = attended + recalled.reshape(length, columns)
    wide = lax.all_to_all(
        combined.astype(jnp.bfloat16), "head", split_axis=0, concat_axis=1, tiled=True
    ).astype(combined.dtype)
    factor = lax.rsqrt(jnp.mean(wide * wide, axis=1, keepdims=True) + EPSILON)
    result = (wide * factor * gain).astype(jnp.bfloat16)
    return result


def solution(mesh):
    in_specs = (
        P(("ctx", "head"), None),
        P(("ctx", "head"), None),
        P(("ctx", "head"), None),
        P(("ctx", "head"), None),
        P(None, "head", None, None),
        P(),
    )
    out_specs = P(("ctx", "head"), None)
    return jax.shard_map(
        on_device, mesh=mesh, in_specs=in_specs, out_specs=out_specs, check_vma=False
    )
```

profile of v0, /device:TPU:0, one launch (start us, length us, event | category | flops | bytes accessed | tf_op | source)
XLA Modules:
  0.0 786.6 jit_solution(563508748399798437)
XLA Ops:
  7.9 7.3 all-to-all-start.3
  33.9 86.4 %all-to-all-done.2 = bf16[256,8,1024]{0,2,1:T(8,128)(2,1)} async-done(((bf16[256,8,1024]{0,2,1:T(8,128)(2,1)}), bf16[256,8,1024]{0,2,1:T(8,128)(2,1)}, u32[]{:S(2)}, u32[]{:S(2)}) %all-to-all-start.2) | async-done | bytes 4194336 | tf_op jit(solution)/shard_map/all_to_all | solution.py:26
  144.8 7.4 concatenate.20
  155.5 61.9 %all-to-all-done = bf16[256,8,1024]{0,2,1:T(8,128)(2,1)} async-done(((bf16[256,8,1024]{0,2,1:T(8,128)(2,1)}), bf16[256,8,1024]{0,2,1:T(8,128)(2,1)}, u32[]{:S(2)}, u32[]{:S(2)}) %all-to-all-start) | async-done | bytes 4194336 | tf_op jit(solution)/shard_map/all_to_all | solution.py:27
  245.6 7.6 concatenate.17
  253.1 7.2 fusion.54
  265.4 8.9 %fusion.45 = f32[1,4,256,256]{3,2,1,0:T(8,128)S(1)} fusion(bf16[2048,4,256]{0,2,1:T(8,128)(2,1)} %concatenate.20, f32[4,2048,256]{2,1,0:T(8,128)} %fusion.39, f32[4,256,2048]{1,2,0:T(8,128)} %fusion.52), kind=kOutput, calls=%fused_computation.69 | convolution fusion | flops 1086324736 | bytes 22020096 | tf_op jit(solution)/shard_map/thf,thd->hfd/dot_general | solution.py:84
  274.2 9.2 %fusion.42 = f32[1,4,256,256]{3,2,1,0:T(8,128)S(1)} fusion(bf16[2048,4,256]{0,2,1:T(8,128)(2,1)} %concatenate.17, f32[2048,4]{0,1:T(4,128)S(1)} %bitcast.169, f32[4,256,2048]{1,2,0:T(8,128)} %fusion.54, f32[4,256,2048]{1,2,0:T(8,128)} %fusion.52), kind=kOutput, calls=%fused_computation.68 | convolution fusion | flops 1092616192 | bytes 22052864 | tf_op jit(solution)/shard_map/thf,thd->hfd/dot_general | solution.py:85
  283.4 11.8 %fusion.48 = f32[1,4,256,256]{3,2,1,0:T(8,128)S(1)} fusion(bf16[2048,4,256]{0,2,1:T(8,128)(2,1)} %concatenate.20, f32[4,256,2048]{1,2,0:T(8,128)} %fusion.52, f32[4,256,2048]{1,2,0:T(8,128)} %fusion.54, f32[4,2048,256]{2,1,0:T(8,128)} %fusion.39), kind=kOutput, calls=%fused_computation.70 | convolution fusion | flops 1094713344 | bytes 30408704 | tf_op jit(solution)/shard_map/thf,thd->hfd/dot_general | solution.py:83
  297.3 17.4 %all-to-all-done.1 = bf16[256,8,1024]{0,2,1:T(8,128)(2,1)} async-done(((bf16[256,8,1024]{0,2,1:T(8,128)(2,1)}), bf16[256,8,1024]{0,2,1:T(8,128)(2,1)}, u32[]{:S(2)}, u32[]{:S(2)}) %all-to-all-start.1) | async-done | bytes 4194336 | tf_op jit(solution)/shard_map/all_to_all | solution.py:25
  321.2 7.4 reshape.171
  341.6 11.7 %pad_maximum_fusion = (bf16[4096,4,256]{0,2,1:T(8,128)(2,1)}, bf16[4096,4,256]{0,2,1:T(8,128)(2,1)}) fusion(bf16[2048,4,256]{0,2,1:T(8,128)(2,1)} %concatenate.17, bf16[2048,4,256]{0,2,1:T(8,128)(2,1)} %bitcast.163, bf16[2048,4,256]{0,2,1:T(8,128)(2,1)} %concatenate.20, bf16[2048,4,256]{0,2,1:T(8,128)(2,1)} %bitcast.162), kind=kLoop, calls=%fused_computation.28 | loop fusion | flops 33554432 | bytes 33554432 | tf_op jit(solution)/shard_map/concatenate | solution.py:41
  353.3 235.3 %while.13 = (s32[]{:T(128)}, f32[4,512,4,256]{3,2,1,0:T(4,128)}, s32[4]{0:T(128)S(1)}, bf16[4096,4,256]{0,2,1:T(8,128)(2,1)}, s32[]{:T(128)}, /*index=5*/bf16[20...) while((s32[]{:T(128)}, f32[4,512,4,256]{3,2,1,0:T(4,128)}, ...), condition=%wide.region_3.4_spmd, body=%wide.region_0.3_spmd.sunk | while | flops 5421149184 | bytes 108578560 | solution.py:66
  354.9 12.8 %fusion.80 = f32[4,512,2560]{2,1,0:T(8,128)} fusion(bf16[4096,4,256]{0,2,1:T(8,128)(2,1)} %get-tuple-element.250, s32[]{:T(128)S(6)} %select_n.45, bf16[2048,4,256]{0,2,1:T(8,128)(2,1)} %get-tuple-element.249, s32[]{:T(128)S(6)} %select_n.46), kind=kOutput, calls=%fused_computation.9.clone.1 | convolution fusion | flops 2684354560 | bytes 27262984 | tf_op jit(solution)/shard_map/while/body/eval_jaxpr/qhd,khd->hqk/dot_general | solution.py:54
  370.6 25.3 %fusion.81 = (f32[4,512]{1,0:T(4,128)S(1)}, f32[4,512,2560]{2,1,0:T(8,128)}) fusion(f32[4,512,2560]{2,1,0:T(8,128)} %fusion.80, pred[512,2560]{1,0:T(8,128)(4,1)S(1)} %and_and_fusion.2), kind=kOutput, calls=%fused_computation.91.clone.1 | output fusion | flops 36702720 | bytes 43261952 | tf_op jit(solution)/shard_map/while/body/eval_jaxpr/sub | solution.py:62
  395.9 12.8 %fusion.82 = f32[1,512,4,256]{1,3,2,0:T(8,128)} fusion(f32[4,512,2560]{2,1,0:T(8,128)} %get-tuple-element.216, f32[4,512]{1,0:T(4,128)S(1)} %get-tuple-element.217, bf16[4096,4,256]{0,2,1:T(8,128)(2,1)} %get-tuple-element.247, s32[]{:T(128)S(6)} %select_n.45), kind=kOutput, calls=%fused_computation.13.clone.1 | convolution fusion | flops 2694840320 | bytes 28319748 | tf_op jit(solution)/shard_map/while/body/eval_jaxpr/hqk,khd->qhd/dot_general | solution.py:64
  413.7 12.7 %fusion.80 = f32[4,512,2560]{2,1,0:T(8,128)} fusion(bf16[4096,4,256]{0,2,1:T(8,128)(2,1)} %get-tuple-element.250, s32[]{:T(128)S(6)} %select_n.45, bf16[2048,4,256]{0,2,1:T(8,128)(2,1)} %get-tuple-element.249, s32[]{:T(128)S(6)} %select_n.46), kind=kOutput, calls=%fused_computation.9.clone.1 | convolution fusion | flops 2684354560 | bytes 27262984 | tf_op jit(solution)/shard_map/while/body/eval_jaxpr/qhd,khd->hqk/dot_general | solution.py:54
  429.3 25.3 %fusion.81 = (f32[4,512]{1,0:T(4,128)S(1)}, f32[4,512,2560]{2,1,0:T(8,128)}) fusion(f32[4,512,2560]{2,1,0:T(8,128)} %fusion.80, pred[512,2560]{1,0:T(8,128)(4,1)S(1)} %and_and_fusion.2), kind=kOutput, calls=%fused_computation.91.clone.1 | output fusion | flops 36702720 | bytes 43261952 | tf_op jit(solution)/shard_map/while/body/eval_jaxpr/sub | solution.py:62
  454.5 12.8 %fusion.82 = f32[1,512,4,256]{1,3,2,0:T(8,128)} fusion(f32[4,512,2560]{2,1,0:T(8,128)} %get-tuple-element.216, f32[4,512]{1,0:T(4,128)S(1)} %get-tuple-element.217, bf16[4096,4,256]{0,2,1:T(8,128)(2,1)} %get-tuple-element.247, s32[]{:T(128)S(6)} %select_n.45), kind=kOutput, calls=%fused_computation.13.clone.1 | convolution fusion | flops 2694840320 | bytes 28319748 | tf_op jit(solution)/shard_map/while/body/eval_jaxpr/hqk,khd->qhd/dot_general | solution.py:64
  472.4 12.7 %fusion.80 = f32[4,512,2560]{2,1,0:T(8,128)} fusion(bf16[4096,4,256]{0,2,1:T(8,128)(2,1)} %get-tuple-element.250, s32[]{:T(128)S(6)} %select_n.45, bf16[2048,4,256]{0,2,1:T(8,128)(2,1)} %get-tuple-element.249, s32[]{:T(128)S(6)} %select_n.46), kind=kOutput, calls=%fused_computation.9.clone.1 | convolution fusion | flops 2684354560 | bytes 27262984 | tf_op jit(solution)/shard_map/while/body/eval_jaxpr/qhd,khd->hqk/dot_general | solution.py:54
  488.0 25.3 %fusion.81 = (f32[4,512]{1,0:T(4,128)S(1)}, f32[4,512,2560]{2,1,0:T(8,128)}) fusion(f32[4,512,2560]{2,1,0:T(8,128)} %fusion.80, pred[512,2560]{1,0:T(8,128)(4,1)S(1)} %and_and_fusion.2), kind=kOutput, calls=%fused_computation.91.clone.1 | output fusion | flops 36702720 | bytes 43261952 | tf_op jit(solution)/shard_map/while/body/eval_jaxpr/sub | solution.py:62
  513.2 12.8 %fusion.82 = f32[1,512,4,256]{1,3,2,0:T(8,128)} fusion(f32[4,512,2560]{2,1,0:T(8,128)} %get-tuple-element.216, f32[4,512]{1,0:T(4,128)S(1)} %get-tuple-element.217, bf16[4096,4,256]{0,2,1:T(8,128)(2,1)} %get-tuple-element.247, s32[]{:T(128)S(6)} %select_n.45), kind=kOutput, calls=%fused_computation.13.clone.1 | convolution fusion | flops 2694840320 | bytes 28319748 | tf_op jit(solution)/shard_map/while/body/eval_jaxpr/hqk,khd->qhd/dot_general | solution.py:64
  531.1 12.7 %fusion.80 = f32[4,512,2560]{2,1,0:T(8,128)} fusion(bf16[4096,4,256]{0,2,1:T(8,128)(2,1)} %get-tuple-element.250, s32[]{:T(128)S(6)} %select_n.45, bf16[2048,4,256]{0,2,1:T(8,128)(2,1)} %get-tuple-element.249, s32[]{:T(128)S(6)} %select_n.46), kind=kOutput, calls=%fused_computation.9.clone.1 | convolution fusion | flops 2684354560 | bytes 27262984 | tf_op jit(solution)/shard_map/while/body/eval_jaxpr/qhd,khd->hqk/dot_general | solution.py:54
  546.7 25.3 %fusion.81 = (f32[4,512]{1,0:T(4,128)S(1)}, f32[4,512,2560]{2,1,0:T(8,128)}) fusion(f32[4,512,2560]{2,1,0:T(8,128)} %fusion.80, pred[512,2560]{1,0:T(8,128)(4,1)S(1)} %and_and_fusion.2), kind=kOutput, calls=%fused_computation.91.clone.1 | output fusion | flops 36702720 | bytes 43261952 | tf_op jit(solution)/shard_map/while/body/eval_jaxpr/sub | solution.py:62
  572.0 12.8 %fusion.82 = f32[1,512,4,256]{1,3,2,0:T(8,128)} fusion(f32[4,512,2560]{2,1,0:T(8,128)} %get-tuple-element.216, f32[4,512]{1,0:T(4,128)S(1)} %get-tuple-element.217, bf16[4096,4,256]{0,2,1:T(8,128)(2,1)} %get-tuple-element.247, s32[]{:T(128)S(6)} %select_n.45), kind=kOutput, calls=%fused_computation.13.clone.1 | convolution fusion | flops 2694840320 | bytes 28319748 | tf_op jit(solution)/shard_map/while/body/eval_jaxpr/hqk,khd->qhd/dot_general | solution.py:64
  588.5 10.9 %reshape.172 = f32[8,256,1024]{2,1,0:T(8,128)} reshape(f32[4,512,4,256]{3,2,1,0:T(4,128)} %get-tuple-element.114) | data formatting | bytes 16777216 | tf_op jit(solution)/shard_map/reshape | solution.py:66
  613.2 11.9 %fusion.41 = f32[4,256,2048]{2,1,0:T(8,128)} fusion(f32[4,256,2048]{1,2,0:T(8,128)} %fusion.51, bf16[2048,4,256]{0,2,1:T(8,128)(2,1)} %get-tuple-element.258, bf16[3,4,256,256]{3,2,1,0:T(8,128)(2,1)S(1)} %multiply_convert_fusion.3), kind=kOutput, calls=%fused_computation.67 | convolution fusion | flops 2160066560 | bytes 22020096 | tf_op jit(solution)/shard_map/thf,hfd->thd/dot_general | solution.py:101
  625.1 10.7 %copy.155 = f32[128,8,8,256]{3,2,1,0:T(8,128)} copy(f32[128,8,8,256]{3,1,2,0:T(8,128)} %bitcast.165) | data formatting | bytes 16777216
  635.8 8.9 %copy.126 = f32[8,256,1024]{2,1,0:T(8,128)} copy(f32[8,256,1024]{1,0,2:T(8,128)} %bitcast.158) | data formatting | bytes 16777216 | tf_op jit(solution)/shard_map/reshape | solution.py:102
  644.7 7.3 add_convert_fusion
  652.0 97.1 %all_to_all.77 = bf16[8,256,1024]{2,1,0:T(8,128)(2,1)S(1)} all-to-all(bf16[8,256,1024]{2,1,0:T(8,128)(2,1)S(1)} %add_convert_fusion), channel_id=1, replica_groups=mesh['ctx'=4,'head'=8] {'head'}, dimensions={0} | all-to-all | bytes 8388608 | tf_op jit(solution)/shard_map/all_to_all | solution.py:103
  755.5 9.2 %copy.127 = f32[256,8,1024]{0,2,1:T(8,128)} copy(f32[256,8,1024]{2,0,1:T(8,128)} %convert_bitcast_fusion) | data formatting | bytes 16777216 | tf_op jit(solution)/shard_map/convert_element_type | solution.py:105
  (81 shorter events, 166.1 us)
Async XLA Ops:
  7.9 13.9 %all-to-all-start.3 = ((bf16[256,8,4]{0,2,1:T(4,128)(2,1)}), bf16[256,8,4]{0,2,1:T(4,128)(2,1)S(1)}, u32[]{:S(2)}, u32[]{:S(2)}) async-start(bf16[256,8,4]{0,2,1:T(4,128)(2,1)} %all_to_all.69), calls=%async_computation.3 | async-start | bytes 32768 | tf_op jit(solution)/shard_map/all_to_all | solution.py:28
  21.7 98.6 %all-to-all-start.2 = ((bf16[256,8,1024]{0,2,1:T(8,128)(2,1)}), bf16[256,8,1024]{0,2,1:T(8,128)(2,1)}, u32[]{:S(2)}, u32[]{:S(2)}) async-start(bf16[256,8,1024]{0,2,1:T(8,128)(2,1)} %bitcast.161), calls=%async_computation.2 | async-start | bytes 8388608 | tf_op jit(solution)/shard_map/all_to_all | solution.py:26
  120.3 97.1 %all-to-all-start = ((bf16[256,8,1024]{0,2,1:T(8,128)(2,1)}), bf16[256,8,1024]{0,2,1:T(8,128)(2,1)}, u32[]{:S(2)}, u32[]{:S(2)}) async-start(bf16[256,8,1024]{0,2,1:T(8,128)(2,1)} %bitcast.160), calls=%async_computation | async-start | bytes 8388608 | tf_op jit(solution)/shard_map/all_to_all | solution.py:27
  152.3 176.4 %collective-permute-start.1 = (bf16[2048,1024]{1,0:T(8,128)(2,1)}, bf16[2048,1024]{1,0:T(8,128)(2,1)}, u32[]{:S(2)}, u32[]{:S(2)}) collective-permute-start(bf16[2048,1024]{1,0:T(8,128)(2,1)} %bitcast.166), channel_id=1, source_target_pairs={{0,8},{8,16},{16,24},{1,9},{9,17},{17,25},{2,10},{10,18},{18,26},{... | collective-permute-start | bytes 12582920 | tf_op jit(solution)/shard_map/ppermute | solution.py:15
  217.4 14.5 %copy-start.3 = (bf16[3,4,256,256]{3,2,1,0:T(8,128)(2,1)S(1)}, bf16[3,4,256,256]{3,2,1,0:T(8,128)(2,1)}, u32[]{:S(2)}) copy-start(bf16[3,4,256,256]{3,2,1,0:T(8,128)(2,1)} %param.12) | copy-start | bytes 4718596
  217.4 97.2 %all-to-all-start.1 = ((bf16[256,8,1024]{0,2,1:T(8,128)(2,1)}), bf16[256,8,1024]{0,2,1:T(8,128)(2,1)}, u32[]{:S(2)}, u32[]{:S(2)}) async-start(bf16[256,8,1024]{0,2,1:T(8,128)(2,1)} %bitcast.159), calls=%async_computation.1 | async-start | bytes 8388608 | tf_op jit(solution)/shard_map/all_to_all | solution.py:25
  222.1 377.4 %all-gather.3.cloned.1.call-start = ((), (), s32[]{:S(2)}) async-start(), calls=%async_computation.5 | async-start | bytes 15728640 | tf_op jit(solution)/shard_map/all_gather | solution.py:89
  228.6 106.5 %collective-permute-start = (bf16[2048,1024]{1,0:T(8,128)(2,1)}, bf16[2048,1024]{1,0:T(8,128)(2,1)}, u32[]{:S(2)}, u32[]{:S(2)}) collective-permute-start(bf16[2048,1024]{1,0:T(8,128)(2,1)} %bitcast.167), channel_id=1, source_target_pairs={{0,8},{8,16},{16,24},{1,9},{9,17},{17,25},{2,10},{10,18},{18,26},{... | collective-permute-start | bytes 12582920 | tf_op jit(solution)/shard_map/ppermute | solution.py:15
  253.1 7.3 copy-start.2
  588.5 11.0 %copy-start.6 = (f32[4]{0:T(128)S(1)}, f32[4]{0:T(128)}, u32[]{:S(2)}) copy-start(f32[4]{0:T(128)} %compare_convert_fusion) | copy-start | bytes 52
  599.5 6.6 copy-start.4
  606.0 2.2 copy-start
  749.2 2.0 copy-start.1
  755.5 12.3 %copy-start.5 = (f32[8192]{0:T(1024)S(1)}, f32[8192]{0:T(1024)}, u32[]{:S(2)}) copy-start(f32[8192]{0:T(1024)} %param.13) | copy-start | bytes 98308
Sparse Core Ops, SparseCore 0:
  297.4 82.4 all-gather.2
where the time goes:
time: 796 us; the launch traced here: 787 us
  matrix products  168 us (21%)
  waiting for transfers between devices  166 us (21%)
  other arithmetic  155 us (19%)
  local copies, waits for them, and re-layouts  154 us (19%)
  blocking collectives  97.1 us (12%)
  starting transfers between devices  29 us (4%)
  between operations  13.8 us (2%)
    sub x4, other arithmetic, attend(): weights = jnp.where(valid, jnp.exp(masked - top), 0.0)  101 us
    all_to_all x1, blocking collectives, on_device(): lax.all_to_all(combined.astype(jnp.bfloat16), 'head', split_axis=0, conca...  97.1 us
    all_to_all x1, waiting for transfers between devices, on_device(): lax.all_to_all(keys, 'head', split_axis=1, concat_axis=0, tiled=True)  86.4 us
    all_to_all x1, waiting for transfers between devices, on_device(): lax.all_to_all(values, 'head', split_axis=1, concat_axis=0, tiled=True)  61.9 us
    dot_general x4, matrix products, attend(): jnp.einsum('hqk,khd->qhd', probs, value_block, preferred_element_type=jnp...  51.4 us
    dot_general x4, matrix products, attend(): jnp.einsum('qhd,khd->hqk', query_block, key_block, preferred_element_type...  51 us
    unnamed x18, local copies, waits for them, and re-layouts  32.2 us
    all_to_all x1, waiting for transfers between devices, on_device(): lax.all_to_all(queries, 'head', split_axis=1, concat_axis=0, tiled=True)  17.4 us
  transfers between devices with their start and end apart: 7, of which 4 were waited for; matrix products, arithmetic and copies ran while one was open for 50% of the time, Pallas kernels for 0%

commit v1 on v0

v1 whole, which is shorter than its diff:
```python
import functools

import jax
import jax.numpy as jnp
from jax import lax
from jax.experimental import pallas as pl
from jax.experimental.pallas import tpu as pltpu
from jax.sharding import PartitionSpec as P

WINDOW = 2048
EPSILON = 1e-06
LOG2E = 1.4426950408889634
NT = (((1,), (1,)), ((), ()))
SUBLANES = 16
PARAMS = pltpu.CompilerParams(vmem_limit_bytes=60 << 20)
COST = 0.001


def dot(a, b):
    return jnp.dot(a, b, preferred_element_type=jnp.float32)


def dot_nt(a, b):
    return lax.dot_general(a, b, NT, preferred_element_type=jnp.float32)


def cost(flops, bytes_accessed, transcendentals=0):
    return pl.CostEstimate(
        flops=int(flops * COST),
        bytes_accessed=int(bytes_accessed * COST),
        transcendentals=int(transcendentals * COST),
    )


def from_behind(value, axis, steps):
    count = lax.axis_size(axis)
    return lax.ppermute(value, axis, [(source, source + steps) for source in range(count - steps)])


def exchange(value):
    return lax.all_to_all(value, "head", split_axis=0, concat_axis=0, tiled=True)


def after(value, earlier):
    return lax.optimization_barrier((value, earlier))[0]


def pack_kernel(*refs, with_rates):
    *sources, out_ref = refs
    rows, size = sources[0].shape[0], out_ref.shape[2]
    at = 0
    if with_rates:
        rate_ref = sources.pop()
        heads = rate_ref.shape[0] // pl.num_programs(0)
        shape = (SUBLANES, rate_ref.shape[0])
        source = lax.broadcasted_iota(jnp.int32, shape, 1)
        target = lax.broadcasted_iota(jnp.int32, shape, 0) + pl.program_id(0) * heads
        chosen = dot((source == target).astype(jnp.bfloat16), rate_ref[...])
        end = out_ref.shape[1]
        out_ref[0, end - SUBLANES : end, :rows] = chosen.astype(jnp.bfloat16)
    for ref in sources:
        for h in range(ref.shape[1] // size):
            out_ref[0, at : at + rows] = ref[:, h * size : (h + 1) * size]
            at += rows


def pack(parts, peers, group, groups, size, rates=None):
    rows = parts[0][0].shape[0]
    specs = [
        pl.BlockSpec((rows, group * size), functools.partial(lambda d, g: (0, d * groups + g), g=g))
        for _, g in parts
    ]
    operands = [array for array, _ in parts]
    count = len(parts) * group * rows
    if rates is not None:
        operands.append(rates)
        specs.append(pl.BlockSpec(rates.shape, lambda d: (0, 0)))
        count += SUBLANES
    return pl.pallas_call(
        functools.partial(pack_kernel, with_rates=rates is not None),
        grid=(peers,),
        in_specs=specs,
        out_specs=pl.BlockSpec((1, count, size), lambda d: (d, 0, 0)),
        out_shape=jax.ShapeDtypeStruct((peers, count, size), jnp.bfloat16),
        compiler_params=PARAMS,
        cost_estimate=cost(0, 4 * peers * count * size),
    )(*operands)


def update_kernel(first_head, k_ref, v_ref, rate_ref, init_ref, out_ref):
    peers, rows, size = k_ref.shape
    head = first_head + pl.program_id(0)
    w_gate, w_up, w_down = init_ref[0, 0], init_ref[1, 0], init_ref[2, 0]
    span = max(1, 512 // rows)
    total = [0.0, 0.0, 0.0]
    for start in range(0, peers, span):
        here = slice(start, start + span)
        tokens = span * rows
        keys = k_ref[here].reshape(tokens, size)
        targets = []
        for s in range(start, start + span):
            turned = jnp.transpose(rate_ref[s].astype(jnp.float32))[:rows]
            lane = lax.broadcasted_iota(jnp.int32, turned.shape, 1)
            rate = jnp.sum(jnp.where(lane == head, turned, 0.0), axis=1, keepdims=True)
            targets.append((rate * v_ref[s].astype(jnp.float32)).astype(jnp.bfloat16))
        targets = jnp.concatenate(targets, axis=0)
        gate_pre = dot_nt(w_gate, keys)
        up_pre = dot_nt(w_up, keys)
        back = dot_nt(w_down, targets)
        sigma = jax.nn.sigmoid(gate_pre)
        gate_act = gate_pre * sigma
        hidden = (gate_act * up_pre).astype(jnp.bfloat16)
        back_gate = (back * up_pre * sigma * (1.0 + gate_pre * (1.0 - sigma))).astype(jnp.bfloat16)
        back_up = (back * gate_act).astype(jnp.bfloat16)
        total[0] += dot(back_gate, keys)
        total[1] += dot(back_up, keys)
        total[2] += dot(hidden, targets)
    for i in range(3):
        out_ref[i, 0] = total[i]


def updates(packed, k_at, v_at, rate_from, fast_init, first_head, group, rows):
    peers, depth, size = rate_from.shape
    hid = fast_init.shape[2]
    length = peers * rows
    block = (peers, rows, size)
    last = depth // SUBLANES - 1
    return pl.pallas_call(
        functools.partial(update_kernel, first_head),
        grid=(group,),
        in_specs=[
            pl.BlockSpec(block, lambda h: (0, k_at + h, 0)),
            pl.BlockSpec(block, lambda h: (0, v_at + h, 0)),
            pl.BlockSpec((peers, SUBLANES, size), lambda h: (0, last, 0)),
            pl.BlockSpec((3, 1, hid, size), lambda h: (0, first_head + h, 0, 0)),
        ],
        out_specs=pl.BlockSpec((3, 1, hid, size), lambda h: (0, h, 0, 0)),
        out_shape=jax.ShapeDtypeStruct((3, group, hid, size), jnp.float32),
        compiler_params=PARAMS,
        cost_estimate=cost(
            group * 6 * 2 * length * size * hid, group * 4 * length * size, group * length * hid
        ),
    )(packed, packed, rate_from, fast_init)


def attend_kernel(place_ref, q_ref, k_ref, v_ref, ek_ref, ev_ref, fit_ref, out_ref):
    peers, rows, size = q_ref.shape
    length = peers * rows
    first = place_ref[0] == 0
    factor = size**-0.5 * LOG2E
    tile = min(256, length)
    span = tile // rows
    flat = lambda ref, low, high: ref[low // rows : high // rows].reshape(high - low, size)
    row = lax.broadcasted_iota(jnp.int32, (tile, tile), 0)
    col = lax.broadcasted_iota(jnp.int32, (tile, tile), 1)
    f_gate, f_up, f_down = fit_ref[0, 0], fit_ref[1, 0], fit_ref[2, 0]
    for start in range(0, length, tile):
        stop = start + tile
        query = flat(q_ref, start, stop)
        far = dot_nt(query, flat(ek_ref, start, length))
        near = dot_nt(query, flat(k_ref, 0, stop))
        far_edge = jnp.where(col > row, far[:, :tile], -jnp.inf)
        near_edge = jnp.where(col <= row, near[:, start:], -jnp.inf)
        far_parts = [far_edge] + ([far[:, tile:]] if far.shape[1] > tile else [])
        near_parts = ([near[:, :start]] if start else []) + [near_edge]
        far = jnp.concatenate(far_parts, axis=1)
        near = jnp.concatenate(near_parts, axis=1)
        top_far = jnp.max(far, axis=1, keepdims=True)
        top_near = jnp.max(near, axis=1, keepdims=True)
        top = jnp.where(first, top_near, jnp.maximum(top_near, top_far))
        shift = top * factor
        shift_far = jnp.where(first, jnp.inf, shift)
        w_far = jnp.exp2(far * factor - shift_far)
        w_near = jnp.exp2(near * factor - shift)
        weight = jnp.sum(w_far, axis=1, keepdims=True) + jnp.sum(w_near, axis=1, keepdims=True)
        attended = dot(w_far.astype(jnp.bfloat16), flat(ev_ref, start, length))
        attended += dot(w_near.astype(jnp.bfloat16), flat(v_ref, 0, stop))
        q_gate = dot_nt(query, f_gate)
        q_up = dot_nt(query, f_up)
        q_hidden = (q_gate * jax.nn.sigmoid(q_gate) * q_up).astype(jnp.bfloat16)
        combined = attended / weight + dot(q_hidden, f_down)
        out_ref[start // rows : stop // rows, 0] = combined.astype(jnp.bfloat16).reshape(
            span, rows, size
        )


def attend(place, q_from, q_at, kv_from, k_at, v_at, edge, ek_at, ev_at, fitted, group, rows):
    peers, _, size = q_from.shape
    hid = fitted.shape[2]
    length = peers * rows
    at = lambda start: pl.BlockSpec((peers, rows, size), lambda h: (0, start + h, 0))
    return pl.pallas_call(
        attend_kernel,
        grid=(group,),
        in_specs=[
            pl.BlockSpec(memory_space=pltpu.SMEM),
            at(q_at),
            at(k_at),
            at(v_at),
            at(ek_at),
            at(ev_at),
            pl.BlockSpec((3, 1, hid, size), lambda h: (0, h, 0, 0)),
        ],
        out_specs=pl.BlockSpec((peers, 1, rows, size), lambda h: (0, h, 0, 0)),
        out_shape=jax.ShapeDtypeStruct((peers, group, rows, size), jnp.bfloat16),
        compiler_params=PARAMS,
        cost_estimate=cost(
            group * length * size * 2 * (2 * (WINDOW + 256) + 3 * hid),
            group * 12 * length * size,
            group * length * (WINDOW + 256),
        ),
    )(place, q_from, kv_from, kv_from, edge, edge, fitted)


def norm_kernel(*refs):
    *sources, gain_ref, out_ref = refs
    peers, group, rows, size = sources[0].shape
    heads = group * len(sources)
    width = out_ref.shape[1]
    square = jnp.zeros((rows, size), jnp.float32)
    for ref in sources:
        for s in range(peers):
            for h in range(group):
                x = ref[s, h].astype(jnp.float32)
                square += x * x
    factor = lax.rsqrt(jnp.sum(square, axis=1, keepdims=True) / width + EPSILON)
    for number, ref in enumerate(sources):
        for s in range(peers):
            for h in range(group):
                low = (s * heads + number * group + h) * size
                x = ref[s, h].astype(jnp.float32)
                out_ref[:, low : low + size] = (
                    x * factor * gain_ref[:, low : low + size]
                ).astype(jnp.bfloat16)


def normalize(parts, gain):
    peers, group, rows, size = parts[0].shape
    width = gain.shape[0]
    step = min(32, rows)
    return pl.pallas_call(
        norm_kernel,
        grid=(rows // step,),
        in_specs=[pl.BlockSpec((peers, group, step, size), lambda i: (0, 0, i, 0)) for _ in parts]
        + [pl.BlockSpec((1, width), lambda i: (0, 0))],
        out_specs=pl.BlockSpec((step, width), lambda i: (i, 0)),
        out_shape=jax.ShapeDtypeStruct((rows, width), jnp.bfloat16),
        compiler_params=PARAMS,
        cost_estimate=cost(5 * rows * width, 4 * rows * width),
    )(*parts, gain.reshape(1, width))


def earlier_sum(value, axis):
    count = lax.axis_size(axis)
    running, before, steps = value, jnp.zeros_like(value), 1
    while steps < count:
        arrived = from_behind(running.astype(jnp.bfloat16), axis, steps).astype(jnp.float32)
        before = before + arrived
        running = running + arrived
        steps *= 2
    return before


def refit(initial, before):
    initial = initial.astype(jnp.float32)
    target_ms = jnp.mean(initial * initial, axis=3, keepdims=True)
    renewed = initial + before
    current = jnp.mean(renewed * renewed, axis=3, keepdims=True)
    return (renewed * jnp.sqrt(target_ms) * lax.rsqrt(current + EPSILON)).astype(jnp.bfloat16)


def on_device(queries, keys, values, rates, fast_init, gain):
    peers = lax.axis_size("head")
    rows = queries.shape[0]
    heads = fast_init.shape[1]
    size = fast_init.shape[3]
    groups = 2
    group = heads // groups
    place = lax.axis_index("ctx").astype(jnp.int32).reshape(1)
    lay = lambda *parts, **more: pack(parts, peers, group, groups, size, **more)

    kv_a = exchange(lay((keys, 0), (values, 0), rates=rates.T))
    kv_a, kvq = lax.optimization_barrier((kv_a, lay((keys, 1), (values, 1), (queries, 0))))
    kvq = exchange(kvq)
    edge_a = from_behind(kv_a, "ctx", 1)
    up_a = updates(kv_a, 0, group, kv_a, fast_init, 0, group, rows)
    fit_a = refit(fast_init[:, :group], earlier_sum(up_a, "ctx"))
    kvq, q_b, fit_a = lax.optimization_barrier((kvq, lay((queries, 1)), fit_a))
    q_b = exchange(q_b)
    kv_b = kvq[:, : 2 * group * rows]
    edge_b = from_behind(kv_b, "ctx", 1)
    up_b = updates(kv_b, 0, group, kv_a, fast_init, group, group, rows)
    fit_b = refit(fast_init[:, group:], earlier_sum(up_b, "ctx"))
    fit_a = after(fit_a, up_b)
    out_a = attend(place, kvq, 2 * group, kv_a, 0, group, edge_a, 0, group, fit_a, group, rows)
    back_a = exchange(after(out_a, q_b))
    out_b = attend(place, q_b, 0, kv_b, 0, group, edge_b, 0, group, fit_b, group, rows)
    back_b = exchange(after(out_b, back_a))
    return normalize([back_a, back_b], gain)


def solution(mesh):
    rows = P(("ctx", "head"), None)
    in_specs = (rows, rows, rows, rows, P(None, "head", None, None), P())
    return jax.shard_map(on_device, mesh=mesh, in_specs=in_specs, out_specs=rows, check_vma=False)
```

time: 796 us -> 421 us (0.53); the launches traced: 787 us -> 420 us
  matrix products: 168 us -> 0 us
  local copies, waits for them, and re-layouts: 154 us -> 4.5 us
  other arithmetic: 155 us -> 6.15 us
  Pallas kernels: 0 us -> 85.4 us
  waiting for transfers between devices: 166 us -> 215 us
  blocking collectives: 97.1 us -> 50.8 us
  starting transfers between devices: 29 us -> 57.6 us
  between operations: 13.8 us -> 0.14 us
    dot_general x16 -> x0, matrix products: 168 us -> none  [the longest x4 51.4 us: attend(): jnp.einsum('hqk,khd->qhd', probs, value_block, preferred_element_type=jnp...]
    sub x4 -> x0, other arithmetic: 101 us -> none  [attend(): weights = jnp.where(valid, jnp.exp(masked - top), 0.0)]
    pallas_call x0 -> x8, Pallas kernels: none -> 85.4 us  [the longest x2 42 us: attend(): pl.pallas_call(attend_kernel, grid=(group,), in_specs=[pl.BlockSpec(memor...]
    all_to_all x1, blocking collectives: 97.1 us -> 50.8 us  [exchange(): lax.all_to_all(value, 'head', split_axis=0, concat_axis=0, tiled=True)]
    all_to_all x6 -> x0, local copies, waits for them, and re-layouts: 33.9 us -> none  [the longest x2 13 us: on_device(): lax.all_to_all(values, 'head', split_axis=1, concat_axis=0, tiled=True)]
    unnamed x18 -> x8, local copies, waits for them, and re-layouts: 32.2 us -> 0.02 us
    ppermute x2 -> x6, starting transfers between devices: 6.5 us -> 36.9 us  [from_behind(): lax.ppermute(value, axis, [(source, source + steps) for source in range(c...]
    reshape x3 -> x0, local copies, waits for them, and re-layouts: 27.3 us -> none  [the longest x1 10.9 us: on_device(): lax.map(attend, jnp.arange(length // block, dtype=jnp.int32))]
  transfers between devices with their start and end apart: 7 -> 10, of which waited for: 4 -> 7; matrix products, arithmetic and copies ran while one was open for 50% -> 3% of each run, Pallas kernels for 0% -> 17%
where the time goes in v1:
time: 421 us; the launch traced here: 420 us
  waiting for transfers between devices  215 us (51%)
  Pallas kernels  85.4 us (20%)
  starting transfers between devices  57.6 us (14%)
  blocking collectives  50.8 us (12%)
  other arithmetic  6.15 us (1%)
  local copies, waits for them, and re-layouts  4.5 us (1%)
    all_to_all x4, waiting for transfers between devices, exchange(): lax.all_to_all(value, 'head', split_axis=0, concat_axis=0, tiled=True)  188 us
    all_to_all x1, blocking collectives, exchange(): lax.all_to_all(value, 'head', split_axis=0, concat_axis=0, tiled=True)  50.8 us
    pallas_call x2, Pallas kernels, attend(): pl.pallas_call(attend_kernel, grid=(group,), in_specs=[pl.BlockSpec(memor...  42 us
    ppermute x6, starting transfers between devices, from_behind(): lax.ppermute(value, axis, [(source, source + steps) for source in range(c...  36.9 us
    ppermute x6, waiting for transfers between devices, from_behind(): lax.ppermute(value, axis, [(source, source + steps) for source in range(c...  26.8 us
    all_to_all x4, starting transfers between devices, exchange(): lax.all_to_all(value, 'head', split_axis=0, concat_axis=0, tiled=True)  20.7 us
    pallas_call x3, Pallas kernels, pack(): pl.pallas_call(functools.partial(pack_kernel, with_rates=rates is not Non...  20.3 us
    pallas_call x2, Pallas kernels, updates(): pl.pallas_call(functools.partial(update_kernel, first_head), grid=(group,...  15.8 us
  transfers between devices with their start and end apart: 10, of which 7 were waited for; matrix products, arithmetic and copies ran while one was open for 3% of the time, Pallas kernels for 17%

profile of v1, /device:TPU:0, one launch (start us, length us, event | category | flops | bytes accessed | tf_op | source)
XLA Modules:
  0.0 419.9 jit_solution(12816734720616099762)
XLA Ops:
  0.0 6.9 %shard_map.64 = bf16[8,1040,256]{2,1,0:T(8,128)(2,1)} custom-call(bf16[256,8192]{1,0:T(8,128)(2,1)} %refs_0_.4, bf16[256,8192]{1,0:T(8,128)(2,1)} %refs_1_.3, bf16[32,256]{1,0:T(8,128)(2,1)} %bitcast.4), custom_call_target="tpu_custom_call" | custom-call | bytes 8519 | tf_op jit(solution)/shard_map/pallas_call | solution.py:79
  6.9 7.3 %all-to-all-start = ((bf16[8,1040,256]{2,1,0:T(8,128)(2,1)}), bf16[8,1040,256]{2,1,0:T(8,128)(2,1)}, u32[]{:S(2)}, u32[]{:S(2)}) async-start(bf16[8,1040,256]{2,1,0:T(8,128)(2,1)} %shard_map.64), calls=%async_computation | async-start | bytes 8519680 | tf_op jit(solution)/shard_map/all_to_all | solution.py:41
  14.2 7.8 %shard_map.65 = bf16[8,1536,256]{2,1,0:T(8,128)(2,1)} custom-call(bf16[256,8192]{1,0:T(8,128)(2,1)} %refs_0_.4, bf16[256,8192]{1,0:T(8,128)(2,1)} %refs_1_.3, bf16[256,8192]{1,0:T(8,128)(2,1)} %refs_0_.5), custom_call_target="tpu_custom_call" | custom-call | bytes 12582 | tf_op jit(solution)/shard_map/pallas_call | solution.py:79
  21.9 86.9 %all-to-all-done.k_ref.v_ref.rate_ref = bf16[8,1040,256]{2,1,0:T(8,128)(2,1)} async-done(((bf16[8,1040,256]{2,1,0:T(8,128)(2,1)}), bf16[8,1040,256]{2,1,0:T(8,128)(2,1)}, u32[]{:S(2)}, u32[]{:S(2)}) %all-to-all-start) | async-done | bytes 4259872 | tf_op jit(solution)/shard_map/all_to_all | solution.py:41
  108.8 4.7 %all-to-all-start.1 = ((bf16[8,1536,256]{2,1,0:T(8,128)(2,1)}), bf16[8,1536,256]{2,1,0:T(8,128)(2,1)}, u32[]{:S(2)}, u32[]{:S(2)}) async-start(bf16[8,1536,256]{2,1,0:T(8,128)(2,1)} %shard_map.65), calls=%async_computation.1 | async-start | bytes 12582912 | tf_op jit(solution)/shard_map/all_to_all | solution.py:41
  113.6 7.9 %shard_map.67 = f32[3,2,256,256]{3,2,1,0:T(8,128)} custom-call(bf16[8,1040,256]{2,1,0:T(8,128)(2,1)} %all-to-all-done.k_ref.v_ref.rate_ref, bf16[8,1040,256]{2,1,0:T(8,128)(2,1)} %all-to-all-done.k_ref.v_ref.rate_ref, bf16[8,1040,256]{2,1,0:T(8,128)(2,1)} %all-to-all-done.k_ref.v_ref.rate_ref, bf16[3,4,256,256]{3,2,1,0:T(8,128)(2,1)} %init_ref.3), custom_call_target="tpu_custom_call" | custom-call | flops 3221225 | bytes 4194 | tf_op jit(solution)/shard_map/pallas_call | solution.py:128
  121.5 1.6 convert_element_type.37
  123.1 1.3 collective-permute-start
  124.5 1.8 collective-permute-done
  126.6 13.7 %collective-permute-start.1 = (bf16[3,2,256,256]{3,2,1,0:T(8,128)(2,1)S(1)}, bf16[3,2,256,256]{3,2,1,0:T(8,128)(2,1)S(1)}, u32[]{:S(2)}, u32[]{:S(2)}) collective-permute-start(bf16[3,2,256,256]{3,2,1,0:T(8,128)(2,1)S(1)} %fusion.1), channel_id=1, source_target_pairs={{0,16},{8,24},{1,17},{9,25},{2,18},{10,26},{3,19},{11,27},{4,20},{... | collective-permute-start | bytes 2359304 | tf_op jit(solution)/shard_map/ppermute | solution.py:37
  140.3 5.7 %shard_map.66 = bf16[8,512,256]{2,1,0:T(8,128)(2,1)} custom-call(bf16[256,8192]{1,0:T(8,128)(2,1)} %refs_0_.5), custom_call_target="tpu_custom_call" | custom-call | bytes 4194 | tf_op jit(solution)/shard_map/pallas_call | solution.py:79
  146.0 3.3 collective-permute-start.2
  149.2 9.0 %collective-permute-done.1 = bf16[3,2,256,256]{3,2,1,0:T(8,128)(2,1)S(1)} collective-permute-done((bf16[3,2,256,256]{3,2,1,0:T(8,128)(2,1)S(1)}, bf16[3,2,256,256]{3,2,1,0:T(8,128)(2,1)S(1)}, u32[]{:S(2)}, u32[]{:S(2)}) %collective-permute-start.1) | collective-permute-done | bytes 786464 | tf_op jit(solution)/shard_map/ppermute | solution.py:37
  158.2 0.8 fusion.2
  159.0 1.4 multiply_convert_fusion.1.fit_ref
  160.4 90.5 %all-to-all-done.1.q_ref = bf16[8,1536,256]{2,1,0:T(8,128)(2,1)} async-done(((bf16[8,1536,256]{2,1,0:T(8,128)(2,1)}), bf16[8,1536,256]{2,1,0:T(8,128)(2,1)}, u32[]{:S(2)}, u32[]{:S(2)}) %all-to-all-start.1) | async-done | bytes 6291488 | tf_op jit(solution)/shard_map/all_to_all | solution.py:41
  250.9 4.4 %all-to-all-start.2 = ((bf16[8,512,256]{2,1,0:T(8,128)(2,1)}), bf16[8,512,256]{2,1,0:T(8,128)(2,1)}, u32[]{:S(2)}, u32[]{:S(2)}) async-start(bf16[8,512,256]{2,1,0:T(8,128)(2,1)} %shard_map.66), calls=%async_computation.2 | async-start | bytes 4194304 | tf_op jit(solution)/shard_map/all_to_all | solution.py:41
  255.3 4.5 %slice.10.k_ref.v_ref = bf16[8,1024,256]{2,1,0:T(8,128)(2,1)} slice(bf16[8,1536,256]{2,1,0:T(8,128)(2,1)} %all-to-all-done.1.q_ref), slice={[0:8], [0:1024], [0:256]} | slice | bytes 8388608 | tf_op jit(solution)/shard_map/slice | solution.py:290
  259.7 3.3 collective-permute-start.3
  263.1 7.9 %shard_map.68 = f32[3,2,256,256]{3,2,1,0:T(8,128)} custom-call(bf16[8,1024,256]{2,1,0:T(8,128)(2,1)} %slice.10.k_ref.v_ref, bf16[8,1024,256]{2,1,0:T(8,128)(2,1)} %slice.10.k_ref.v_ref, bf16[8,1040,256]{2,1,0:T(8,128)(2,1)} %all-to-all-done.k_ref.v_ref.rate_ref, bf16[3,4,256,256]{3,2,1,0:T(8,128)(2,1)} %init_ref.3), custom_call_target="tpu_custom_call" | custom-call | flops 3221225 | bytes 4194 | tf_op jit(solution)/shard_map/pallas_call | solution.py:128
  271.0 21.0 %shard_map.69 = bf16[8,2,256,256]{3,2,1,0:T(8,128)(2,1)} custom-call(s32[1]{0:T(128)} %bitcast.place_ref, bf16[8,1536,256]{2,1,0:T(8,128)(2,1)} %all-to-all-done.1.q_ref, bf16[8,1040,256]{2,1,0:T(8,128)(2,1)} %all-to-all-done.k_ref.v_ref.rate_ref, bf16[8,1040,256]{2,1,0:T(8,128)(2,1)} %all-to-all-done.k_ref.v_ref.rate_ref, ...), custom_call_target="tpu_custom_call" | custom-call | flops 11274289 | bytes 12582 | tf_op jit(solution)/shard_map/pallas_call | solution.py:192
  292.0 11.0 %all-to-all-done.2.q_ref = bf16[8,512,256]{2,1,0:T(8,128)(2,1)} async-done(((bf16[8,512,256]{2,1,0:T(8,128)(2,1)}), bf16[8,512,256]{2,1,0:T(8,128)(2,1)}, u32[]{:S(2)}, u32[]{:S(2)}) %all-to-all-start.2) | async-done | bytes 2097184 | tf_op jit(solution)/shard_map/all_to_all | solution.py:41
  303.0 4.3 %all-to-all-start.3 = ((bf16[8,2,256,256]{3,2,1,0:T(8,128)(2,1)}), bf16[8,2,256,256]{3,2,1,0:T(8,128)(2,1)}, u32[]{:S(2)}, u32[]{:S(2)}) async-start(bf16[8,2,256,256]{3,2,1,0:T(8,128)(2,1)} %shard_map.69), calls=%async_computation.3 | async-start | bytes 4194304 | tf_op jit(solution)/shard_map/all_to_all | solution.py:41
  307.5 1.5 collective-permute-start.4
  309.0 1.8 collective-permute-done.4
  311.0 13.8 %collective-permute-start.5 = (bf16[3,2,256,256]{3,2,1,0:T(8,128)(2,1)S(1)}, bf16[3,2,256,256]{3,2,1,0:T(8,128)(2,1)S(1)}, u32[]{:S(2)}, u32[]{:S(2)}) collective-permute-start(bf16[3,2,256,256]{3,2,1,0:T(8,128)(2,1)S(1)} %fusion.3), channel_id=1, source_target_pairs={{0,16},{8,24},{1,17},{9,25},{2,18},{10,26},{3,19},{11,27},{4,20},{... | collective-permute-start | bytes 2359304 | tf_op jit(solution)/shard_map/ppermute | solution.py:37
  324.9 14.2 %collective-permute-done.5 = bf16[3,2,256,256]{3,2,1,0:T(8,128)(2,1)S(1)} collective-permute-done((bf16[3,2,256,256]{3,2,1,0:T(8,128)(2,1)S(1)}, bf16[3,2,256,256]{3,2,1,0:T(8,128)(2,1)S(1)}, u32[]{:S(2)}, u32[]{:S(2)}) %collective-permute-start.5) | collective-permute-done | bytes 786464 | tf_op jit(solution)/shard_map/ppermute | solution.py:37
  339.0 0.4 multiply_reduce_fusion
  339.5 1.4 multiply_convert_fusion.fit_ref
  340.9 21.0 %shard_map.70 = bf16[8,2,256,256]{3,2,1,0:T(8,128)(2,1)} custom-call(s32[1]{0:T(128)} %bitcast.place_ref, bf16[8,512,256]{2,1,0:T(8,128)(2,1)} %all-to-all-done.2.q_ref, bf16[8,1024,256]{2,1,0:T(8,128)(2,1)} %slice.10.k_ref.v_ref, bf16[8,1024,256]{2,1,0:T(8,128)(2,1)} %slice.10.k_ref.v_ref, bf16[8,1024,256]{2,1,0:T(8,128)(2,1)} %collective-permute-done.3.ek_ref.ev_ref, ...), custom_call_target="tpu_custom_call" | custom-call | flops 11274289 | bytes 12582 | tf_op jit(solution)/shard_map/pallas_call | solution.py:192
  361.8 50.8 %all_to_all.25.refs_1_ = bf16[8,2,256,256]{3,2,1,0:T(8,128)(2,1)} all-to-all(bf16[8,2,256,256]{3,2,1,0:T(8,128)(2,1)} %shard_map.70), channel_id=1, replica_groups=mesh['ctx'=4,'head'=8] {'head'}, dimensions={0} | all-to-all | bytes 4194304 | tf_op jit(solution)/shard_map/all_to_all | solution.py:41
  412.6 7.3 %shard_map.71 = bf16[256,8192]{1,0:T(8,128)(2,1)} custom-call(bf16[8,2,256,256]{3,2,1,0:T(8,128)(2,1)} %all-to-all-done.3.refs_0_, bf16[8,2,256,256]{3,2,1,0:T(8,128)(2,1)} %all_to_all.25.refs_1_, f32[1,8192]{1,0:T(1,128)} %bitcast.3), custom_call_target="tpu_custom_call" | custom-call | flops 10485 | bytes 8388 | tf_op jit(solution)/shard_map/pallas_call | solution.py:241
  (17 shorter events, 0.6 us)
Async XLA Ops:
  6.9 102.0 %all-to-all-start = ((bf16[8,1040,256]{2,1,0:T(8,128)(2,1)}), bf16[8,1040,256]{2,1,0:T(8,128)(2,1)}, u32[]{:S(2)}, u32[]{:S(2)}) async-start(bf16[8,1040,256]{2,1,0:T(8,128)(2,1)} %shard_map.64), calls=%async_computation | async-start | bytes 8519680 | tf_op jit(solution)/shard_map/all_to_all | solution.py:41
  108.8 142.1 %all-to-all-start.1 = ((bf16[8,1536,256]{2,1,0:T(8,128)(2,1)}), bf16[8,1536,256]{2,1,0:T(8,128)(2,1)}, u32[]{:S(2)}, u32[]{:S(2)}) async-start(bf16[8,1536,256]{2,1,0:T(8,128)(2,1)} %shard_map.65), calls=%async_computation.1 | async-start | bytes 12582912 | tf_op jit(solution)/shard_map/all_to_all | solution.py:41
  121.5 4.8 %copy-start.3 = (f32[3,2,256,256]{3,2,1,0:T(8,128)S(1)}, f32[3,2,256,256]{3,2,1,0:T(8,128)}, u32[]{:S(2)}) copy-start(f32[3,2,256,256]{3,2,1,0:T(8,128)} %shard_map.67) | copy-start | bytes 4718596
  123.1 3.2 collective-permute-start
  126.5 31.7 %copy-start = (bf16[3,4,256,256]{3,2,1,0:T(8,128)(2,1)S(1)}, bf16[3,4,256,256]{3,2,1,0:T(8,128)(2,1)}, u32[]{:S(2)}) copy-start(bf16[3,4,256,256]{3,2,1,0:T(8,128)(2,1)} %init_ref.3) | copy-start | bytes 4718596
  126.6 31.6 %collective-permute-start.1 = (bf16[3,2,256,256]{3,2,1,0:T(8,128)(2,1)S(1)}, bf16[3,2,256,256]{3,2,1,0:T(8,128)(2,1)S(1)}, u32[]{:S(2)}, u32[]{:S(2)}) collective-permute-start(bf16[3,2,256,256]{3,2,1,0:T(8,128)(2,1)S(1)} %fusion.1), channel_id=1, source_target_pairs={{0,16},{8,24},{1,17},{9,25},{2,18},{10,26},{3,19},{11,27},{4,20},{... | collective-permute-start | bytes 2359304 | tf_op jit(solution)/shard_map/ppermute | solution.py:37
  146.0 125.0 %collective-permute-start.2 = (bf16[8,1040,256]{2,1,0:T(8,128)(2,1)}, bf16[8,1040,256]{2,1,0:T(8,128)(2,1)}, u32[]{:S(2)}, u32[]{:S(2)}) collective-permute-start(bf16[8,1040,256]{2,1,0:T(8,128)(2,1)} %all-to-all-done.k_ref.v_ref.rate_ref), channel_id=1, source_target_pairs={{0,8},{8,16},{16,24},{1,9},{9,17},{17,25},{2,10},{10,18},{18,26},{... | collective-permute-start | bytes 12779528 | tf_op jit(solution)/shard_map/ppermute | solution.py:37
  250.9 52.1 %all-to-all-start.2 = ((bf16[8,512,256]{2,1,0:T(8,128)(2,1)}), bf16[8,512,256]{2,1,0:T(8,128)(2,1)}, u32[]{:S(2)}, u32[]{:S(2)}) async-start(bf16[8,512,256]{2,1,0:T(8,128)(2,1)} %shard_map.66), calls=%async_computation.2 | async-start | bytes 4194304 | tf_op jit(solution)/shard_map/all_to_all | solution.py:41
  259.7 81.1 %collective-permute-start.3 = (bf16[8,1024,256]{2,1,0:T(8,128)(2,1)}, bf16[8,1024,256]{2,1,0:T(8,128)(2,1)}, u32[]{:S(2)}, u32[]{:S(2)}) collective-permute-start(bf16[8,1024,256]{2,1,0:T(8,128)(2,1)} %slice.10.k_ref.v_ref), channel_id=1, source_target_pairs={{0,8},{8,16},{16,24},{1,9},{9,17},{17,25},{2,10},{10,18},{18,26},{... | collective-permute-start | bytes 12582920 | tf_op jit(solution)/shard_map/ppermute | solution.py:37
  292.0 15.4 %copy-start.2 = (f32[3,2,256,256]{3,2,1,0:T(8,128)S(1)}, f32[3,2,256,256]{3,2,1,0:T(8,128)}, u32[]{:S(2)}) copy-start(f32[3,2,256,256]{3,2,1,0:T(8,128)} %shard_map.68) | copy-start | bytes 4718596
  303.0 58.8 %all-to-all-start.3 = ((bf16[8,2,256,256]{3,2,1,0:T(8,128)(2,1)}), bf16[8,2,256,256]{3,2,1,0:T(8,128)(2,1)}, u32[]{:S(2)}, u32[]{:S(2)}) async-start(bf16[8,2,256,256]{3,2,1,0:T(8,128)(2,1)} %shard_map.69), calls=%async_computation.3 | async-start | bytes 4194304 | tf_op jit(solution)/shard_map/all_to_all | solution.py:41
  307.5 31.6 %copy-start.1 = (bf16[3,4,256,256]{3,2,1,0:T(8,128)(2,1)S(1)}, bf16[3,4,256,256]{3,2,1,0:T(8,128)(2,1)}, u32[]{:S(2)}) copy-start(bf16[3,4,256,256]{3,2,1,0:T(8,128)(2,1)} %init_ref.3) | copy-start | bytes 4718596
  307.5 3.3 collective-permute-start.4
  311.0 28.0 %collective-permute-start.5 = (bf16[3,2,256,256]{3,2,1,0:T(8,128)(2,1)S(1)}, bf16[3,2,256,256]{3,2,1,0:T(8,128)(2,1)S(1)}, u32[]{:S(2)}, u32[]{:S(2)}) collective-permute-start(bf16[3,2,256,256]{3,2,1,0:T(8,128)(2,1)S(1)} %fusion.3), channel_id=1, source_target_pairs={{0,16},{8,24},{1,17},{9,25},{2,18},{10,26},{3,19},{11,27},{4,20},{... | collective-permute-start | bytes 2359304 | tf_op jit(solution)/shard_map/ppermute | solution.py:37

commit v2 on v1

--- a/solution.py
+++ b/solution.py
@@ -45,43 +45,77 @@
     return lax.optimization_barrier((value, earlier))[0]
 
 
-def pack_kernel(*refs, with_rates):
-    *sources, out_ref = refs
-    rows, size = sources[0].shape[0], out_ref.shape[2]
-    at = 0
-    if with_rates:
-        rate_ref = sources.pop()
-        heads = rate_ref.shape[0] // pl.num_programs(0)
-        shape = (SUBLANES, rate_ref.shape[0])
+def pack_kernel(pieces, group, groups, rate_ref, *refs):
+    sources = refs[: len(pieces)]
+    out_ref, held, came, went = refs[len(pieces) : len(pieces) + 4]
+    peers, _, size = out_ref.shape
+    rows = held.shape[1]
+    inward, outward = [], []
+    for d in range(peers):
+        at = 0
+        for ref, g in zip(sources, pieces):
+            for h in range(group):
+                n = len(inward)
+                column = ((d * groups + g) * group + h) * size
+                source = ref.at[:, pl.ds(column, size)]
+                inward.append(pltpu.make_async_copy(source, held.at[n], came.at[n]))
+                target = out_ref.at[d, pl.ds(at, rows)]
+                outward.append(pltpu.make_async_copy(held.at[n], target, went.at[n]))
+                at += rows
+    for copy in inward:
+        copy.start()
+    extra = []
+    if rate_ref is not None:
+        turned, sent = refs[len(pieces) + 4 :]
+        heads = rate_ref.shape[0] // peers
+        shape = (peers * SUBLANES, rate_ref.shape[0])
+        slot = lax.broadcasted_iota(jnp.int32, shape, 0)
         source = lax.broadcasted_iota(jnp.int32, shape, 1)
-        target = lax.broadcasted_iota(jnp.int32, shape, 0) + pl.program_id(0) * heads
-        chosen = dot((source == target).astype(jnp.bfloat16), rate_ref[...])
-        end = out_ref.shape[1]
-        out_ref[0, end - SUBLANES : end, :rows] = chosen.astype(jnp.bfloat16)
-    for ref in sources:
-        for h in range(ref.shape[1] // size):
-            out_ref[0, at : at + rows] = ref[:, h * size : (h + 1) * size]
-            at += rows
+        chosen = dot(
+            (source == slot // SUBLANES * heads + slot % SUBLANES).astype(jnp.bfloat16),
+            rate_ref[...],
+        )
+        turned[:, :, :rows] = chosen.astype(jnp.bfloat16).reshape(peers, SUBLANES, rows)
+        for d in range(peers):
+            target = out_ref.at[d, pl.ds(at, SUBLANES)]
+            extra.append(pltpu.make_async_copy(turned.at[d], target, sent.at[d]))
+            extra[-1].start()
+    for before, behind in zip(inward, outward):
+        before.wait()
+        behind.start()
+    for copy in outward + extra:
+        copy.wait()
 
 
 def pack(parts, peers, group, groups, size, rates=None):
     rows = parts[0][0].shape[0]
-    specs = [
-        pl.BlockSpec((rows, group * size), functools.partial(lambda d, g: (0, d * groups + g), g=g))
-        for _, g in parts
+    operands = [array for array, _ in parts]
+    pieces = [g for _, g in parts]
+    copies = peers * len(parts) * group
+    count = len(parts) * group * rows
+    specs = [pl.BlockSpec(memory_space=pl.ANY) for _ in parts]
+    scratch = [
+        pltpu.VMEM((copies, rows, size), jnp.bfloat16),
+        pltpu.SemaphoreType.DMA((copies,)),
+        pltpu.SemaphoreType.DMA((copies,)),
     ]
-    operands = [array for array, _ in parts]
-    count = len(parts) * group * rows
-    if rates is not None:
-        operands.append(rates)
-        specs.append(pl.BlockSpec(rates.shape, lambda d: (0, 0)))
+    body = functools.partial(pack_kernel, pieces, group, groups)
+    if rates is None:
+        body = functools.partial(body, None)
+    else:
+        operands.insert(0, rates)
+        specs.insert(0, pl.BlockSpec(memory_space=pltpu.VMEM))
         count += SUBLANES
+        scratch += [
+            pltpu.VMEM((peers, SUBLANES, size), jnp.bfloat16),
+            pltpu.SemaphoreType.DMA((peers,)),
+        ]
     return pl.pallas_call(
-        functools.partial(pack_kernel, with_rates=rates is not None),
-        grid=(peers,),
+        body,
         in_specs=specs,
-        out_specs=pl.BlockSpec((1, count, size), lambda d: (d, 0, 0)),
+        out_specs=pl.BlockSpec(memory_space=pl.ANY),
         out_shape=jax.ShapeDtypeStruct((peers, count, size), jnp.bfloat16),
+        scratch_shapes=scratch,
         compiler_params=PARAMS,
         cost_estimate=cost(0, 4 * peers * count * size),
     )(*operands)
@@ -237,7 +271,7 @@
 def normalize(parts, gain):
     peers, group, rows, size = parts[0].shape
     width = gain.shape[0]
-    step = min(32, rows)
+    step = min(128, rows)
     return pl.pallas_call(
         norm_kernel,
         grid=(rows // step,),
@@ -251,13 +285,10 @@
 
 
 def earlier_sum(value, axis):
-    count = lax.axis_size(axis)
-    running, before, steps = value, jnp.zeros_like(value), 1
-    while steps < count:
-        arrived = from_behind(running.astype(jnp.bfloat16), axis, steps).astype(jnp.float32)
-        before = before + arrived
-        running = running + arrived
-        steps *= 2
+    before = jnp.zeros_like(value)
+    for step in range(1, lax.axis_size(axis)):
+        running = (value + before).astype(jnp.bfloat16)
+        before = before + lax.ppermute(running, axis, [(step - 1, step)]).astype(jnp.float32)
     return before
 
 

time: 421 us -> 411 us (0.976)
  starting transfers between devices: 57.6 us -> 44.8 us
  Pallas kernels: 85.4 us -> 76.6 us
  waiting for transfers between devices: 215 us -> 223 us
    all_to_all x4, waiting for transfers between devices: 188 us -> 221 us  [exchange(): lax.all_to_all(value, 'head', split_axis=0, concat_axis=0, tiled=True)]
    ppermute x6 -> x2, waiting for transfers between devices: 26.8 us -> 0.01 us  [from_behind(): lax.ppermute(value, axis, [(source, source + steps) for source in range(c...]
    ppermute x6 -> x2, starting transfers between devices: 36.9 us -> 17.1 us  [from_behind(): lax.ppermute(value, axis, [(source, source + steps) for source in range(c...]
    ppermute x0 -> x6, starting transfers between devices: none -> 7.03 us  [earlier_sum(): lax.ppermute(running, axis, [(step - 1, step)]).astype(jnp.float32)]
    pallas_call x3, Pallas kernels: 20.3 us -> 14.2 us  [pack(): pl.pallas_call(body, in_specs=specs, out_specs=pl.BlockSpec(memory_space=...]
  transfers between devices with their start and end apart: 10 -> 12, of which waited for: 7 -> 5; matrix products, arithmetic and copies ran while one was open for 3% -> 3% of each run, Pallas kernels for 17% -> 16%
where the time goes in v2:
time: 411 us
  waiting for transfers between devices  223 us (54%)
  Pallas kernels  76.6 us (19%)
  blocking collectives  52.2 us (13%)
  starting transfers between devices  44.8 us (11%)
  other arithmetic  9.26 us (2%)
  local copies, waits for them, and re-layouts  4.49 us (1%)
    all_to_all x4, waiting for transfers between devices, exchange(): lax.all_to_all(value, 'head', split_axis=0, concat_axis=0, tiled=True)  221 us
    all_to_all x1, blocking collectives, exchange(): lax.all_to_all(value, 'head', split_axis=0, concat_axis=0, tiled=True)  52.2 us
    pallas_call x2, Pallas kernels, attend(): pl.pallas_call(attend_kernel, grid=(group,), in_specs=[pl.BlockSpec(memor...  42 us
    all_to_all x4, starting transfers between devices, exchange(): lax.all_to_all(value, 'head', split_axis=0, concat_axis=0, tiled=True)  20.8 us
    ppermute x2, starting transfers between devices, from_behind(): lax.ppermute(value, axis, [(source, source + steps) for source in range(c...  17.1 us
    pallas_call x2, Pallas kernels, updates(): pl.pallas_call(functools.partial(update_kernel, first_head), grid=(group,...  15.8 us
    pallas_call x3, Pallas kernels, pack(): pl.pallas_call(body, in_specs=specs, out_specs=pl.BlockSpec(memory_space=...  14.2 us
  transfers between devices with their start and end apart: 12, of which 5 were waited for; matrix products, arithmetic and copies ran while one was open for 3% of the time, Pallas kernels for 16%

profile of v2, /device:TPU:0, one launch (start us, length us, event | category | flops | bytes accessed | tf_op | source)
XLA Modules:
  0.0 410.7 jit_solution(10524944602606748444)
XLA Ops:
  0.0 5.5 %shard_map.64 = bf16[8,1040,256]{2,1,0:T(8,128)(2,1)} custom-call(bf16[32,256]{1,0:T(8,128)(2,1)} %bitcast.4, bf16[256,8192]{1,0:T(8,128)(2,1)} %refs_0_.4, bf16[256,8192]{1,0:T(8,128)(2,1)} %refs_1_.3), custom_call_target="tpu_custom_call" | custom-call | bytes 8519 | tf_op jit(solution)/shard_map/pallas_call | solution.py:113
  5.5 7.3 %all-to-all-start = ((bf16[8,1040,256]{2,1,0:T(8,128)(2,1)}), bf16[8,1040,256]{2,1,0:T(8,128)(2,1)}, u32[]{:S(2)}, u32[]{:S(2)}) async-start(bf16[8,1040,256]{2,1,0:T(8,128)(2,1)} %shard_map.64), calls=%async_computation | async-start | bytes 8519680 | tf_op jit(solution)/shard_map/all_to_all | solution.py:41
  12.8 6.0 %shard_map.65 = bf16[8,1536,256]{2,1,0:T(8,128)(2,1)} custom-call(bf16[256,8192]{1,0:T(8,128)(2,1)} %refs_0_.4, bf16[256,8192]{1,0:T(8,128)(2,1)} %refs_1_.3, bf16[256,8192]{1,0:T(8,128)(2,1)} %refs_0_.5), custom_call_target="tpu_custom_call" | custom-call | bytes 12582 | tf_op jit(solution)/shard_map/pallas_call | solution.py:113
  18.8 88.7 %all-to-all-done.k_ref.v_ref.rate_ref = bf16[8,1040,256]{2,1,0:T(8,128)(2,1)} async-done(((bf16[8,1040,256]{2,1,0:T(8,128)(2,1)}), bf16[8,1040,256]{2,1,0:T(8,128)(2,1)}, u32[]{:S(2)}, u32[]{:S(2)}) %all-to-all-start) | async-done | bytes 4259872 | tf_op jit(solution)/shard_map/all_to_all | solution.py:41
  107.5 4.8 %all-to-all-start.1 = ((bf16[8,1536,256]{2,1,0:T(8,128)(2,1)}), bf16[8,1536,256]{2,1,0:T(8,128)(2,1)}, u32[]{:S(2)}, u32[]{:S(2)}) async-start(bf16[8,1536,256]{2,1,0:T(8,128)(2,1)} %shard_map.65), calls=%async_computation.1 | async-start | bytes 12582912 | tf_op jit(solution)/shard_map/all_to_all | solution.py:41
  112.2 7.9 %shard_map.67 = f32[3,2,256,256]{3,2,1,0:T(8,128)} custom-call(bf16[8,1040,256]{2,1,0:T(8,128)(2,1)} %all-to-all-done.k_ref.v_ref.rate_ref, bf16[8,1040,256]{2,1,0:T(8,128)(2,1)} %all-to-all-done.k_ref.v_ref.rate_ref, bf16[8,1040,256]{2,1,0:T(8,128)(2,1)} %all-to-all-done.k_ref.v_ref.rate_ref, bf16[3,4,256,256]{3,2,1,0:T(8,128)(2,1)} %init_ref.3), custom_call_target="tpu_custom_call" | custom-call | flops 3221225 | bytes 4194 | tf_op jit(solution)/shard_map/pallas_call | solution.py:162
  120.1 1.6 convert_element_type.49
  121.8 1.3 collective-permute-start
  123.1 1.8 collective-permute-done
  125.2 0.7 collective-permute-start.1
  125.9 1.2 add_convert_fusion.1
  127.2 0.8 collective-permute-start.2
  128.0 2.7 shard_map.66
  130.7 13.7 %collective-permute-start.3 = (bf16[8,1040,256]{2,1,0:T(8,128)(2,1)}, bf16[8,1040,256]{2,1,0:T(8,128)(2,1)}, u32[]{:S(2)}, u32[]{:S(2)}) collective-permute-start(bf16[8,1040,256]{2,1,0:T(8,128)(2,1)} %all-to-all-done.k_ref.v_ref.rate_ref), channel_id=1, source_target_pairs={{0,8},{8,16},{16,24},{1,9},{9,17},{17,25},{2,10},{10,18},{18,26},{... | collective-permute-start | bytes 12779528 | tf_op jit(solution)/shard_map/ppermute | solution.py:37
  145.1 1.4 multiply_convert_fusion.1.fit_ref
  146.5 103.0 %all-to-all-done.1.q_ref = bf16[8,1536,256]{2,1,0:T(8,128)(2,1)} async-done(((bf16[8,1536,256]{2,1,0:T(8,128)(2,1)}), bf16[8,1536,256]{2,1,0:T(8,128)(2,1)}, u32[]{:S(2)}, u32[]{:S(2)}) %all-to-all-start.1) | async-done | bytes 6291488 | tf_op jit(solution)/shard_map/all_to_all | solution.py:41
  249.5 4.4 %all-to-all-start.2 = ((bf16[8,512,256]{2,1,0:T(8,128)(2,1)}), bf16[8,512,256]{2,1,0:T(8,128)(2,1)}, u32[]{:S(2)}, u32[]{:S(2)}) async-start(bf16[8,512,256]{2,1,0:T(8,128)(2,1)} %shard_map.66), calls=%async_computation.2 | async-start | bytes 4194304 | tf_op jit(solution)/shard_map/all_to_all | solution.py:41
  253.9 4.5 %slice.10.k_ref.v_ref = bf16[8,1024,256]{2,1,0:T(8,128)(2,1)} slice(bf16[8,1536,256]{2,1,0:T(8,128)(2,1)} %all-to-all-done.1.q_ref), slice={[0:8], [0:1024], [0:256]} | slice | bytes 8388608 | tf_op jit(solution)/shard_map/slice | solution.py:321
  258.4 3.3 collective-permute-start.4
  261.7 7.9 %shard_map.68 = f32[3,2,256,256]{3,2,1,0:T(8,128)} custom-call(bf16[8,1024,256]{2,1,0:T(8,128)(2,1)} %slice.10.k_ref.v_ref, bf16[8,1024,256]{2,1,0:T(8,128)(2,1)} %slice.10.k_ref.v_ref, bf16[8,1040,256]{2,1,0:T(8,128)(2,1)} %all-to-all-done.k_ref.v_ref.rate_ref, bf16[3,4,256,256]{3,2,1,0:T(8,128)(2,1)} %init_ref.3), custom_call_target="tpu_custom_call" | custom-call | flops 3221225 | bytes 4194 | tf_op jit(solution)/shard_map/pallas_call | solution.py:162
  269.6 1.5 convert_element_type.57
  271.1 2.4 collective-permute-start.5
  273.5 21.0 %shard_map.69 = bf16[8,2,256,256]{3,2,1,0:T(8,128)(2,1)} custom-call(s32[1]{0:T(128)} %bitcast.place_ref, bf16[8,1536,256]{2,1,0:T(8,128)(2,1)} %all-to-all-done.1.q_ref, bf16[8,1040,256]{2,1,0:T(8,128)(2,1)} %all-to-all-done.k_ref.v_ref.rate_ref, bf16[8,1040,256]{2,1,0:T(8,128)(2,1)} %all-to-all-done.k_ref.v_ref.rate_ref, ...), custom_call_target="tpu_custom_call" | custom-call | flops 11274289 | bytes 12582 | tf_op jit(solution)/shard_map/pallas_call | solution.py:226
  294.5 7.2 %all-to-all-done.2.q_ref = bf16[8,512,256]{2,1,0:T(8,128)(2,1)} async-done(((bf16[8,512,256]{2,1,0:T(8,128)(2,1)}), bf16[8,512,256]{2,1,0:T(8,128)(2,1)}, u32[]{:S(2)}, u32[]{:S(2)}) %all-to-all-start.2) | async-done | bytes 2097184 | tf_op jit(solution)/shard_map/all_to_all | solution.py:41
  301.7 4.4 %all-to-all-start.3 = ((bf16[8,2,256,256]{3,2,1,0:T(8,128)(2,1)}), bf16[8,2,256,256]{3,2,1,0:T(8,128)(2,1)}, u32[]{:S(2)}, u32[]{:S(2)}) async-start(bf16[8,2,256,256]{3,2,1,0:T(8,128)(2,1)} %shard_map.69), calls=%async_computation.3 | async-start | bytes 4194304 | tf_op jit(solution)/shard_map/all_to_all | solution.py:41
  306.2 0.8 collective-permute-start.6
  307.4 0.9 collective-permute-start.7
  309.1 1.4 multiply_convert_fusion.fit_ref
  310.5 21.0 %shard_map.70 = bf16[8,2,256,256]{3,2,1,0:T(8,128)(2,1)} custom-call(s32[1]{0:T(128)} %bitcast.place_ref, bf16[8,512,256]{2,1,0:T(8,128)(2,1)} %all-to-all-done.2.q_ref, bf16[8,1024,256]{2,1,0:T(8,128)(2,1)} %slice.10.k_ref.v_ref, bf16[8,1024,256]{2,1,0:T(8,128)(2,1)} %slice.10.k_ref.v_ref, bf16[8,1024,256]{2,1,0:T(8,128)(2,1)} %collective-permute-done.4.ek_ref.ev_ref, ...), custom_call_target="tpu_custom_call" | custom-call | flops 11274289 | bytes 12582 | tf_op jit(solution)/shard_map/pallas_call | solution.py:226
  331.5 22.3 %all-to-all-done.3.refs_0_ = bf16[8,2,256,256]{3,2,1,0:T(8,128)(2,1)} async-done(((bf16[8,2,256,256]{3,2,1,0:T(8,128)(2,1)}), bf16[8,2,256,256]{3,2,1,0:T(8,128)(2,1)}, u32[]{:S(2)}, u32[]{:S(2)}) %all-to-all-start.3) | async-done | bytes 2097184 | tf_op jit(solution)/shard_map/all_to_all | solution.py:41
  353.8 52.2 %all_to_all.25.refs_1_ = bf16[8,2,256,256]{3,2,1,0:T(8,128)(2,1)} all-to-all(bf16[8,2,256,256]{3,2,1,0:T(8,128)(2,1)} %shard_map.70), channel_id=1, replica_groups=mesh['ctx'=4,'head'=8] {'head'}, dimensions={0} | all-to-all | bytes 4194304 | tf_op jit(solution)/shard_map/all_to_all | solution.py:41
  406.1 4.7 %shard_map.71 = bf16[256,8192]{1,0:T(8,128)(2,1)} custom-call(bf16[8,2,256,256]{3,2,1,0:T(8,128)(2,1)} %all-to-all-done.3.refs_0_, bf16[8,2,256,256]{3,2,1,0:T(8,128)(2,1)} %all_to_all.25.refs_1_, f32[1,8192]{1,0:T(1,128)} %bitcast.3), custom_call_target="tpu_custom_call" | custom-call | flops 10485 | bytes 8388 | tf_op jit(solution)/shard_map/pallas_call | solution.py:275
  (23 shorter events, 2.2 us)
Async XLA Ops:
  5.5 102.0 %all-to-all-start = ((bf16[8,1040,256]{2,1,0:T(8,128)(2,1)}), bf16[8,1040,256]{2,1,0:T(8,128)(2,1)}, u32[]{:S(2)}, u32[]{:S(2)}) async-start(bf16[8,1040,256]{2,1,0:T(8,128)(2,1)} %shard_map.64), calls=%async_computation | async-start | bytes 8519680 | tf_op jit(solution)/shard_map/all_to_all | solution.py:41
  107.5 142.0 %all-to-all-start.1 = ((bf16[8,1536,256]{2,1,0:T(8,128)(2,1)}), bf16[8,1536,256]{2,1,0:T(8,128)(2,1)}, u32[]{:S(2)}, u32[]{:S(2)}) async-start(bf16[8,1536,256]{2,1,0:T(8,128)(2,1)} %shard_map.65), calls=%async_computation.1 | async-start | bytes 12582912 | tf_op jit(solution)/shard_map/all_to_all | solution.py:41
  120.1 4.8 %copy-start.1 = (f32[3,2,256,256]{3,2,1,0:T(8,128)S(1)}, f32[3,2,256,256]{3,2,1,0:T(8,128)}, u32[]{:S(2)}) copy-start(f32[3,2,256,256]{3,2,1,0:T(8,128)} %shard_map.67) | copy-start | bytes 4718596
  121.8 3.2 collective-permute-start
  125.2 0.7 collective-permute-start.1
  127.1 17.3 %copy-start.2 = (bf16[3,4,256,256]{3,2,1,0:T(8,128)(2,1)S(1)}, bf16[3,4,256,256]{3,2,1,0:T(8,128)(2,1)}, u32[]{:S(2)}) copy-start(bf16[3,4,256,256]{3,2,1,0:T(8,128)(2,1)} %init_ref.3) | copy-start | bytes 4718596
  127.2 17.3 %collective-permute-start.2 = (bf16[3,2,256,256]{3,2,1,0:T(8,128)(2,1)}, bf16[3,2,256,256]{3,2,1,0:T(8,128)(2,1)S(1)}, u32[]{:S(2)}, u32[]{:S(2)}) collective-permute-start(bf16[3,2,256,256]{3,2,1,0:T(8,128)(2,1)} %add_convert_fusion.1), channel_id=1, source_target_pairs={{16,24},{17,25},{18,26},{19,27},{20,28},{21,29},{22,30},{23,31}} | collective-permute-start | bytes 2359304 | tf_op jit(solution)/shard_map/ppermute | solution.py:291
  130.7 142.8 %collective-permute-start.3 = (bf16[8,1040,256]{2,1,0:T(8,128)(2,1)}, bf16[8,1040,256]{2,1,0:T(8,128)(2,1)}, u32[]{:S(2)}, u32[]{:S(2)}) collective-permute-start(bf16[8,1040,256]{2,1,0:T(8,128)(2,1)} %all-to-all-done.k_ref.v_ref.rate_ref), channel_id=1, source_target_pairs={{0,8},{8,16},{16,24},{1,9},{9,17},{17,25},{2,10},{10,18},{18,26},{... | collective-permute-start | bytes 12779528 | tf_op jit(solution)/shard_map/ppermute | solution.py:37
  249.5 52.1 %all-to-all-start.2 = ((bf16[8,512,256]{2,1,0:T(8,128)(2,1)}), bf16[8,512,256]{2,1,0:T(8,128)(2,1)}, u32[]{:S(2)}, u32[]{:S(2)}) async-start(bf16[8,512,256]{2,1,0:T(8,128)(2,1)} %shard_map.66), calls=%async_computation.2 | async-start | bytes 4194304 | tf_op jit(solution)/shard_map/all_to_all | solution.py:41
  258.4 52.1 %collective-permute-start.4 = (bf16[8,1024,256]{2,1,0:T(8,128)(2,1)}, bf16[8,1024,256]{2,1,0:T(8,128)(2,1)}, u32[]{:S(2)}, u32[]{:S(2)}) collective-permute-start(bf16[8,1024,256]{2,1,0:T(8,128)(2,1)} %slice.10.k_ref.v_ref), channel_id=1, source_target_pairs={{0,8},{8,16},{16,24},{1,9},{9,17},{17,25},{2,10},{10,18},{18,26},{... | collective-permute-start | bytes 12582920 | tf_op jit(solution)/shard_map/ppermute | solution.py:37
  271.1 35.0 %collective-permute-start.5 = (bf16[3,2,256,256]{3,2,1,0:T(8,128)(2,1)S(1)}, bf16[3,2,256,256]{3,2,1,0:T(8,128)(2,1)S(1)}, u32[]{:S(2)}, u32[]{:S(2)}) collective-permute-start(bf16[3,2,256,256]{3,2,1,0:T(8,128)(2,1)S(1)} %convert_element_type.57), channel_id=1, source_target_pairs={{0,8},{1,9},{2,10},{3,11},{4,12},{5,13},{6,14},{7,15}} | collective-permute-start | bytes 2359304 | tf_op jit(solution)/shard_map/ppermute | solution.py:291
  294.5 11.6 %copy-start = (f32[3,2,256,256]{3,2,1,0:T(8,128)S(1)}, f32[3,2,256,256]{3,2,1,0:T(8,128)}, u32[]{:S(2)}) copy-start(f32[3,2,256,256]{3,2,1,0:T(8,128)} %shard_map.68) | copy-start | bytes 4718596
  301.7 52.2 %all-to-all-start.3 = ((bf16[8,2,256,256]{3,2,1,0:T(8,128)(2,1)}), bf16[8,2,256,256]{3,2,1,0:T(8,128)(2,1)}, u32[]{:S(2)}, u32[]{:S(2)}) async-start(bf16[8,2,256,256]{3,2,1,0:T(8,128)(2,1)} %shard_map.69), calls=%async_computation.3 | async-start | bytes 4194304 | tf_op jit(solution)/shard_map/all_to_all | solution.py:41
  306.2 2.2 copy-start.3
  306.2 0.9 collective-permute-start.6
  307.4 0.9 collective-permute-start.7

commit v3 on v2

--- a/solution.py
+++ b/solution.py
@@ -177,7 +177,7 @@
     )(packed, packed, rate_from, fast_init)
 
 
-def attend_kernel(place_ref, q_ref, k_ref, v_ref, ek_ref, ev_ref, fit_ref, out_ref):
+def attend_kernel(place_ref, q_ref, k_ref, v_ref, ek_ref, ev_ref, fit_ref, *refs):
     peers, rows, size = q_ref.shape
     length = peers * rows
     first = place_ref[0] == 0
@@ -213,12 +213,17 @@
         q_up = dot_nt(query, f_up)
         q_hidden = (q_gate * jax.nn.sigmoid(q_gate) * q_up).astype(jnp.bfloat16)
         combined = attended / weight + dot(q_hidden, f_down)
-        out_ref[start // rows : stop // rows, 0] = combined.astype(jnp.bfloat16).reshape(
-            span, rows, size
-        )
-
-
-def attend(place, q_from, q_at, kv_from, k_at, v_at, edge, ek_at, ev_at, fitted, group, rows):
+        combined = combined.astype(jnp.bfloat16).reshape(span, rows, size)
+        if len(refs) == 1:
+            refs[0][start // rows : stop // rows, 0] = combined
+        else:
+            for n in range(span):
+                refs[-1][place_ref[1] ^ (start // rows + n)] = combined[n]
+    for step, out_ref in enumerate(refs[:-1]):
+        out_ref[0] = refs[-1][step]
+
+
+def attend(place, q_from, q_at, kv_from, k_at, v_at, edge, ek_at, ev_at, fitted, group, rows, split):
     peers, _, size = q_from.shape
     hid = fitted.shape[2]
     length = peers * rows
@@ -235,8 +240,13 @@
             at(ev_at),
             pl.BlockSpec((3, 1, hid, size), lambda h: (0, h, 0, 0)),
         ],
-        out_specs=pl.BlockSpec((peers, 1, rows, size), lambda h: (0, h, 0, 0)),
-        out_shape=jax.ShapeDtypeStruct((peers, group, rows, size), jnp.bfloat16),
+        out_specs=[pl.BlockSpec((1, rows, size), lambda h: (h, 0, 0))] * peers
+        if split
+        else pl.BlockSpec((peers, 1, rows, size), lambda h: (0, h, 0, 0)),
+        out_shape=[jax.ShapeDtypeStruct((group, rows, size), jnp.bfloat16)] * peers
+        if split
+        else jax.ShapeDtypeStruct((peers, group, rows, size), jnp.bfloat16),
+        scratch_shapes=[pltpu.VMEM((peers, rows, size), jnp.bfloat16)] if split else [],
         compiler_params=PARAMS,
         cost_estimate=cost(
             group * length * size * 2 * (2 * (WINDOW + 256) + 3 * hid),
@@ -246,48 +256,64 @@
     )(place, q_from, kv_from, kv_from, edge, edge, fitted)
 
 
-def norm_kernel(*refs):
-    *sources, gain_ref, out_ref = refs
-    peers, group, rows, size = sources[0].shape
-    heads = group * len(sources)
+def swap_order(count):
+    short = [step for step in (1, 2) if step < count]
+    return short + list(range(count - 1, 2, -1)) + [0]
+
+
+def swap(pieces):
+    count = lax.axis_size("head")
+    return [
+        lax.ppermute(pieces[step], "head", [(i, i ^ step) for i in range(count)])
+        if step
+        else pieces[0]
+        for step in swap_order(count)
+    ]
+
+
+def norm_kernel(place_ref, first_ref, *refs):
+    *pieces, gain_ref, out_ref = refs
+    peers, group, rows, size = first_ref.shape
     width = out_ref.shape[1]
+    parts = [(lambda p=p, h=h: first_ref[p, h], p * 2 * group + h) for p in range(peers) for h in range(group)]
+    for step, ref in zip(swap_order(peers), pieces):
+        p = place_ref[1] ^ step
+        parts += [(lambda ref=ref, h=h: ref[h], (p * 2 + 1) * group + h) for h in range(group)]
     square = jnp.zeros((rows, size), jnp.float32)
-    for ref in sources:
-        for s in range(peers):
-            for h in range(group):
-                x = ref[s, h].astype(jnp.float32)
-                square += x * x
+    for load, _ in parts:
+        x = load().astype(jnp.float32)
+        square += x * x
     factor = lax.rsqrt(jnp.sum(square, axis=1, keepdims=True) / width + EPSILON)
-    for number, ref in enumerate(sources):
-        for s in range(peers):
-            for h in range(group):
-                low = (s * heads + number * group + h) * size
-                x = ref[s, h].astype(jnp.float32)
-                out_ref[:, low : low + size] = (
-                    x * factor * gain_ref[:, low : low + size]
-                ).astype(jnp.bfloat16)
-
-
-def normalize(parts, gain):
-    peers, group, rows, size = parts[0].shape
+    for load, head in parts:
+        here = pl.ds(pl.multiple_of(head * size, size), size)
+        x = load().astype(jnp.float32)
+        out_ref[:, here] = (x * factor * gain_ref[:, here]).astype(jnp.bfloat16)
+
+
+def normalize(place, first, pieces, gain):
+    peers, group, rows, size = first.shape
     width = gain.shape[0]
     step = min(128, rows)
     return pl.pallas_call(
         norm_kernel,
         grid=(rows // step,),
-        in_specs=[pl.BlockSpec((peers, group, step, size), lambda i: (0, 0, i, 0)) for _ in parts]
+        in_specs=[
+            pl.BlockSpec(memory_space=pltpu.SMEM),
+            pl.BlockSpec((peers, group, step, size), lambda i: (0, 0, i, 0)),
+        ]
+        + [pl.BlockSpec((group, step, size), lambda i: (0, i, 0)) for _ in pieces]
         + [pl.BlockSpec((1, width), lambda i: (0, 0))],
         out_specs=pl.BlockSpec((step, width), lambda i: (i, 0)),
         out_shape=jax.ShapeDtypeStruct((rows, width), jnp.bfloat16),
         compiler_params=PARAMS,
         cost_estimate=cost(5 * rows * width, 4 * rows * width),
-    )(*parts, gain.reshape(1, width))
-
-
-def earlier_sum(value, axis):
+    )(place, first, *pieces, gain.reshape(1, width))
+
+
+def earlier_sum(value, axis, dtype):
     before = jnp.zeros_like(value)
     for step in range(1, lax.axis_size(axis)):
-        running = (value + before).astype(jnp.bfloat16)
+        running = (value + before).astype(dtype)
         before = before + lax.ppermute(running, axis, [(step - 1, step)]).astype(jnp.float32)
     return before
 
@@ -307,7 +333,7 @@
     size = fast_init.shape[3]
     groups = 2
     group = heads // groups
-    place = lax.axis_index("ctx").astype(jnp.int32).reshape(1)
+    place = jnp.stack([lax.axis_index("ctx"), lax.axis_index("head")]).astype(jnp.int32)
     lay = lambda *parts, **more: pack(parts, peers, group, groups, size, **more)
 
     kv_a = exchange(lay((keys, 0), (values, 0), rates=rates.T))
@@ -315,19 +341,18 @@
     kvq = exchange(kvq)
     edge_a = from_behind(kv_a, "ctx", 1)
     up_a = updates(kv_a, 0, group, kv_a, fast_init, 0, group, rows)
-    fit_a = refit(fast_init[:, :group], earlier_sum(up_a, "ctx"))
+    fit_a = refit(fast_init[:, :group], earlier_sum(up_a, "ctx", jnp.float32))
     kvq, q_b, fit_a = lax.optimization_barrier((kvq, lay((queries, 1)), fit_a))
     q_b = exchange(q_b)
     kv_b = kvq[:, : 2 * group * rows]
     edge_b = from_behind(kv_b, "ctx", 1)
     up_b = updates(kv_b, 0, group, kv_a, fast_init, group, group, rows)
-    fit_b = refit(fast_init[:, group:], earlier_sum(up_b, "ctx"))
+    fit_b = refit(fast_init[:, group:], earlier_sum(up_b, "ctx", jnp.bfloat16))
     fit_a = after(fit_a, up_b)
-    out_a = attend(place, kvq, 2 * group, kv_a, 0, group, edge_a, 0, group, fit_a, group, rows)
+    out_a = attend(place, kvq, 2 * group, kv_a, 0, group, edge_a, 0, group, fit_a, group, rows, False)
     back_a = exchange(after(out_a, q_b))
-    out_b = attend(place, q_b, 0, kv_b, 0, group, edge_b, 0, group, fit_b, group, rows)
-    back_b = exchange(after(out_b, back_a))
-    return normalize([back_a, back_b], gain)
+    out_b = attend(place, q_b, 0, kv_b, 0, group, edge_b, 0, group, fit_b, group, rows, True)
+    return normalize(place, back_a, swap(out_b), gain)
 
 
 def solution(mesh):

time: 411 us -> 405 us (0.985)
  blocking collectives: 52.2 us -> 0 us
  starting transfers between devices: 44.8 us -> 67.5 us
  waiting for transfers between devices: 223 us -> 242 us
    ppermute x0 -> x7, waiting for transfers between devices: none -> 54.1 us  [swap(): lax.ppermute(pieces[step], 'head', [(i, i ^ step) for i in range(count)])]
    all_to_all x1 -> x0, blocking collectives: 52.2 us -> none  [exchange(): lax.all_to_all(value, 'head', split_axis=0, concat_axis=0, tiled=True)]
    all_to_all x4, waiting for transfers between devices: 221 us -> 184 us  [exchange(): lax.all_to_all(value, 'head', split_axis=0, concat_axis=0, tiled=True)]
    ppermute x0 -> x7, starting transfers between devices: none -> 13 us  [swap(): lax.ppermute(pieces[step], 'head', [(i, i ^ step) for i in range(count)])]
    ppermute x2, starting transfers between devices: 17.1 us -> 25.5 us  [from_behind(): lax.ppermute(value, axis, [(source, source + steps) for source in range(c...]
  transfers between devices with their start and end apart: 12 -> 19, of which waited for: 5 -> 10; matrix products, arithmetic and copies ran while one was open for 3% -> 4% of each run, Pallas kernels for 16% -> 17%
where the time goes in v3:
time: 405 us; the launch traced here: 404 us
  waiting for transfers between devices  242 us (60%)
  Pallas kernels  76.9 us (19%)
  starting transfers between devices  67.5 us (17%)
  other arithmetic  12.5 us (3%)
  local copies, waits for them, and re-layouts  5.25 us (1%)
    all_to_all x4, waiting for transfers between devices, exchange(): lax.all_to_all(value, 'head', split_axis=0, concat_axis=0, tiled=True)  184 us
    ppermute x7, waiting for transfers between devices, swap(): lax.ppermute(pieces[step], 'head', [(i, i ^ step) for i in range(count)])  54.1 us
    pallas_call x2, Pallas kernels, attend(): pl.pallas_call(attend_kernel, grid=(group,), in_specs=[pl.BlockSpec(memor...  42.3 us
    ppermute x2, starting transfers between devices, from_behind(): lax.ppermute(value, axis, [(source, source + steps) for source in range(c...  25.5 us
    all_to_all x4, starting transfers between devices, exchange(): lax.all_to_all(value, 'head', split_axis=0, concat_axis=0, tiled=True)  20.7 us
    pallas_call x2, Pallas kernels, updates(): pl.pallas_call(functools.partial(update_kernel, first_head), grid=(group,...  15.8 us
    pallas_call x3, Pallas kernels, pack(): pl.pallas_call(body, in_specs=specs, out_specs=pl.BlockSpec(memory_space=...  14.2 us
    ppermute x7, starting transfers between devices, swap(): lax.ppermute(pieces[step], 'head', [(i, i ^ step) for i in range(count)])  13 us
  transfers between devices with their start and end apart: 19, of which 10 were waited for; matrix products, arithmetic and copies ran while one was open for 4% of the time, Pallas kernels for 17%

profile of v3, /device:TPU:0, one launch (start us, length us, event | category | flops | bytes accessed | tf_op | source)
XLA Modules:
  0.0 404.2 jit_solution(11680811290509972347)
XLA Ops:
  0.0 5.5 %shard_map.64 = bf16[8,1040,256]{2,1,0:T(8,128)(2,1)} custom-call(bf16[32,256]{1,0:T(8,128)(2,1)} %bitcast.5, bf16[256,8192]{1,0:T(8,128)(2,1)} %refs_0_.4, bf16[256,8192]{1,0:T(8,128)(2,1)} %refs_1_.3), custom_call_target="tpu_custom_call" | custom-call | bytes 8519 | tf_op jit(solution)/shard_map/pallas_call | solution.py:113
  5.5 7.3 %all-to-all-start = ((bf16[8,1040,256]{2,1,0:T(8,128)(2,1)}), bf16[8,1040,256]{2,1,0:T(8,128)(2,1)}, u32[]{:S(2)}, u32[]{:S(2)}) async-start(bf16[8,1040,256]{2,1,0:T(8,128)(2,1)} %shard_map.64), calls=%async_computation | async-start | bytes 8519680 | tf_op jit(solution)/shard_map/all_to_all | solution.py:41
  12.8 6.0 %shard_map.65 = bf16[8,1536,256]{2,1,0:T(8,128)(2,1)} custom-call(bf16[256,8192]{1,0:T(8,128)(2,1)} %refs_0_.4, bf16[256,8192]{1,0:T(8,128)(2,1)} %refs_1_.3, bf16[256,8192]{1,0:T(8,128)(2,1)} %refs_0_.5), custom_call_target="tpu_custom_call" | custom-call | bytes 12582 | tf_op jit(solution)/shard_map/pallas_call | solution.py:113
  18.8 88.7 %all-to-all-done.k_ref.v_ref.rate_ref = bf16[8,1040,256]{2,1,0:T(8,128)(2,1)} async-done(((bf16[8,1040,256]{2,1,0:T(8,128)(2,1)}), bf16[8,1040,256]{2,1,0:T(8,128)(2,1)}, u32[]{:S(2)}, u32[]{:S(2)}) %all-to-all-start) | async-done | bytes 4259872 | tf_op jit(solution)/shard_map/all_to_all | solution.py:41
  107.5 4.8 %all-to-all-start.1 = ((bf16[8,1536,256]{2,1,0:T(8,128)(2,1)}), bf16[8,1536,256]{2,1,0:T(8,128)(2,1)}, u32[]{:S(2)}, u32[]{:S(2)}) async-start(bf16[8,1536,256]{2,1,0:T(8,128)(2,1)} %shard_map.65), calls=%async_computation.1 | async-start | bytes 12582912 | tf_op jit(solution)/shard_map/all_to_all | solution.py:41
  112.3 7.9 %shard_map.67 = f32[3,2,256,256]{3,2,1,0:T(8,128)} custom-call(bf16[8,1040,256]{2,1,0:T(8,128)(2,1)} %all-to-all-done.k_ref.v_ref.rate_ref, bf16[8,1040,256]{2,1,0:T(8,128)(2,1)} %all-to-all-done.k_ref.v_ref.rate_ref, bf16[8,1040,256]{2,1,0:T(8,128)(2,1)} %all-to-all-done.k_ref.v_ref.rate_ref, bf16[3,4,256,256]{3,2,1,0:T(8,128)(2,1)} %init_ref.3), custom_call_target="tpu_custom_call" | custom-call | flops 3221225 | bytes 4194 | tf_op jit(solution)/shard_map/pallas_call | solution.py:162
  120.2 1.5 collective-permute-start
  121.7 3.1 collective-permute-done
  124.8 1.6 add.46
  128.7 1.9 collective-permute-start.2
  130.6 2.7 shard_map.66
  133.3 22.1 %collective-permute-start.3 = (bf16[8,1040,256]{2,1,0:T(8,128)(2,1)}, bf16[8,1040,256]{2,1,0:T(8,128)(2,1)}, u32[]{:S(2)}, u32[]{:S(2)}) collective-permute-start(bf16[8,1040,256]{2,1,0:T(8,128)(2,1)} %all-to-all-done.k_ref.v_ref.rate_ref), channel_id=1, source_target_pairs={{0,8},{8,16},{16,24},{1,9},{9,17},{17,25},{2,10},{10,18},{18,26},{... | collective-permute-start | bytes 12779528 | tf_op jit(solution)/shard_map/ppermute | solution.py:37
  155.5 2.1 fusion.1
  157.6 2.8 multiply_convert_fusion.1.fit_ref
  160.4 89.2 %all-to-all-done.1.q_ref = bf16[8,1536,256]{2,1,0:T(8,128)(2,1)} async-done(((bf16[8,1536,256]{2,1,0:T(8,128)(2,1)}), bf16[8,1536,256]{2,1,0:T(8,128)(2,1)}, u32[]{:S(2)}, u32[]{:S(2)}) %all-to-all-start.1) | async-done | bytes 6291488 | tf_op jit(solution)/shard_map/all_to_all | solution.py:41
  249.6 4.3 %all-to-all-start.2 = ((bf16[8,512,256]{2,1,0:T(8,128)(2,1)}), bf16[8,512,256]{2,1,0:T(8,128)(2,1)}, u32[]{:S(2)}, u32[]{:S(2)}) async-start(bf16[8,512,256]{2,1,0:T(8,128)(2,1)} %shard_map.66), calls=%async_computation.2 | async-start | bytes 4194304 | tf_op jit(solution)/shard_map/all_to_all | solution.py:41
  253.9 4.5 %slice.10.k_ref.v_ref = bf16[8,1024,256]{2,1,0:T(8,128)(2,1)} slice(bf16[8,1536,256]{2,1,0:T(8,128)(2,1)} %all-to-all-done.1.q_ref), slice={[0:8], [0:1024], [0:256]} | slice | bytes 8388608 | tf_op jit(solution)/shard_map/slice | solution.py:347
  258.4 3.4 collective-permute-start.4
  261.7 7.9 %shard_map.68 = f32[3,2,256,256]{3,2,1,0:T(8,128)} custom-call(bf16[8,1024,256]{2,1,0:T(8,128)(2,1)} %slice.10.k_ref.v_ref, bf16[8,1024,256]{2,1,0:T(8,128)(2,1)} %slice.10.k_ref.v_ref, bf16[8,1040,256]{2,1,0:T(8,128)(2,1)} %all-to-all-done.k_ref.v_ref.rate_ref, bf16[3,4,256,256]{3,2,1,0:T(8,128)(2,1)} %init_ref.3), custom_call_target="tpu_custom_call" | custom-call | flops 3221225 | bytes 4194 | tf_op jit(solution)/shard_map/pallas_call | solution.py:162
  271.1 2.3 collective-permute-start.5
  274.0 21.1 %shard_map.69 = bf16[8,2,256,256]{3,2,1,0:T(8,128)(2,1)} custom-call(s32[2]{0:T(128)} %pad_add_fusion.place_ref, bf16[8,1536,256]{2,1,0:T(8,128)(2,1)} %all-to-all-done.1.q_ref, bf16[8,1040,256]{2,1,0:T(8,128)(2,1)} %all-to-all-done.k_ref.v_ref.rate_ref, bf16[8,1040,256]{2,1,0:T(8,128)(2,1)} %all-to-all-done.k_ref.v_ref.rate_ref, ...), custom_call_target="tpu_custom_call" | custom-call | flops 11274289 | bytes 12582 | tf_op jit(solution)/shard_map/pallas_call | solution.py:231
  295.1 6.6 %all-to-all-done.2.q_ref = bf16[8,512,256]{2,1,0:T(8,128)(2,1)} async-done(((bf16[8,512,256]{2,1,0:T(8,128)(2,1)}), bf16[8,512,256]{2,1,0:T(8,128)(2,1)}, u32[]{:S(2)}, u32[]{:S(2)}) %all-to-all-start.2) | async-done | bytes 2097184 | tf_op jit(solution)/shard_map/all_to_all | solution.py:41
  301.7 4.3 %all-to-all-start.3 = ((bf16[8,2,256,256]{3,2,1,0:T(8,128)(2,1)}), bf16[8,2,256,256]{3,2,1,0:T(8,128)(2,1)}, u32[]{:S(2)}, u32[]{:S(2)}) async-start(bf16[8,2,256,256]{3,2,1,0:T(8,128)(2,1)} %shard_map.69), calls=%async_computation.3 | async-start | bytes 4194304 | tf_op jit(solution)/shard_map/all_to_all | solution.py:41
  310.4 21.2 %shard_map.70 = (bf16[2,256,256]{2,1,0:T(8,128)(2,1)}, bf16[2,256,256]{2,1,0:T(8,128)(2,1)}, bf16[2,256,256]{2,1,0:T(8,128)(2,1)}, bf16[2,256,256]{2,1,0:T(8,128...) custom-call(s32[2]{0:T(128)} %pad_add_fusion.place_ref, ...), custom_call_target="tpu_custom_call" | custom-call | flops 11274289 | bytes 12582 | tf_op jit(solution)/shard_map/pallas_call | solution.py:231
  331.6 1.9 collective-permute-start.8
  335.0 2.4 collective-permute-start.10
  342.9 3.2 collective-permute-start.14
  346.1 4.3 %collective-permute-done.10.refs_2_ = bf16[2,256,256]{2,1,0:T(8,128)(2,1)S(1)} collective-permute-done((bf16[2,256,256]{2,1,0:T(8,128)(2,1)}, bf16[2,256,256]{2,1,0:T(8,128)(2,1)S(1)}, u32[]{:S(2)}, u32[]{:S(2)}) %collective-permute-start.10) | collective-permute-done | bytes 262176 | tf_op jit(solution)/shard_map/ppermute | solution.py:267
  350.4 3.9 collective-permute-done.11.refs_3_
  354.3 40.7 %collective-permute-done.12.refs_4_ = bf16[2,256,256]{2,1,0:T(8,128)(2,1)S(1)} collective-permute-done((bf16[2,256,256]{2,1,0:T(8,128)(2,1)}, bf16[2,256,256]{2,1,0:T(8,128)(2,1)S(1)}, u32[]{:S(2)}, u32[]{:S(2)}) %collective-permute-start.12) | collective-permute-done | bytes 262176 | tf_op jit(solution)/shard_map/ppermute | solution.py:267
  395.0 3.7 collective-permute-done.13.refs_5_
  399.5 4.6 %shard_map.71 = bf16[256,8192]{1,0:T(8,128)(2,1)} custom-call(s32[2]{0:T(128)} %pad_add_fusion.place_ref, bf16[8,2,256,256]{3,2,1,0:T(8,128)(2,1)} %all-to-all-done.3.first_ref, bf16[2,256,256]{2,1,0:T(8,128)(2,1)} %copy-done.4, bf16[2,256,256]{2,1,0:T(8,128)(2,1)} %copy-done.5, bf16[2,256,256]{2,1,0:T(8,128)(2,1)} %copy-done.6, ...), custom_call_target="tpu_custom_call" | custom-call | flops 10485 | bytes 8388 | tf_op jit(solution)/shard_map/pallas_call | solution.py:297
  (50 shorter events, 16.3 us)
Async XLA Ops:
  5.5 102.0 %all-to-all-start = ((bf16[8,1040,256]{2,1,0:T(8,128)(2,1)}), bf16[8,1040,256]{2,1,0:T(8,128)(2,1)}, u32[]{:S(2)}, u32[]{:S(2)}) async-start(bf16[8,1040,256]{2,1,0:T(8,128)(2,1)} %shard_map.64), calls=%async_computation | async-start | bytes 8519680 | tf_op jit(solution)/shard_map/all_to_all | solution.py:41
  107.5 142.0 %all-to-all-start.1 = ((bf16[8,1536,256]{2,1,0:T(8,128)(2,1)}), bf16[8,1536,256]{2,1,0:T(8,128)(2,1)}, u32[]{:S(2)}, u32[]{:S(2)}) async-start(bf16[8,1536,256]{2,1,0:T(8,128)(2,1)} %shard_map.65), calls=%async_computation.1 | async-start | bytes 12582912 | tf_op jit(solution)/shard_map/all_to_all | solution.py:41
  120.2 7.0 %copy-start.3 = (f32[3,2,256,256]{3,2,1,0:T(8,128)S(1)}, f32[3,2,256,256]{3,2,1,0:T(8,128)}, u32[]{:S(2)}) copy-start(f32[3,2,256,256]{3,2,1,0:T(8,128)} %shard_map.67) | copy-start | bytes 4718596
  120.2 4.6 %collective-permute-start = (f32[3,2,256,256]{3,2,1,0:T(8,128)}, f32[3,2,256,256]{3,2,1,0:T(8,128)S(1)}, u32[]{:S(2)}, u32[]{:S(2)}) collective-permute-start(f32[3,2,256,256]{3,2,1,0:T(8,128)} %shard_map.67), channel_id=1, source_target_pairs={{0,8},{1,9},{2,10},{3,11},{4,12},{5,13},{6,14},{7,15}} | collective-permute-start | bytes 4718600 | tf_op jit(solution)/shard_map/ppermute | solution.py:317
  126.4 0.8 collective-permute-start.1
  128.7 26.8 %copy-start = (bf16[3,4,256,256]{3,2,1,0:T(8,128)(2,1)S(1)}, bf16[3,4,256,256]{3,2,1,0:T(8,128)(2,1)}, u32[]{:S(2)}) copy-start(bf16[3,4,256,256]{3,2,1,0:T(8,128)(2,1)} %init_ref.3) | copy-start | bytes 4718596
  128.7 26.8 %collective-permute-start.2 = (f32[3,2,256,256]{3,2,1,0:T(8,128)}, f32[3,2,256,256]{3,2,1,0:T(8,128)}, u32[]{:S(2)}, u32[]{:S(2)}) collective-permute-start(f32[3,2,256,256]{3,2,1,0:T(8,128)} %get-tuple-element.38), channel_id=1, source_target_pairs={{16,24},{17,25},{18,26},{19,27},{20,28},{21,29},{22,30},{23,31}} | collective-permute-start | bytes 4718600 | tf_op jit(solution)/shard_map/ppermute | solution.py:317
  133.3 140.7 %collective-permute-start.3 = (bf16[8,1040,256]{2,1,0:T(8,128)(2,1)}, bf16[8,1040,256]{2,1,0:T(8,128)(2,1)}, u32[]{:S(2)}, u32[]{:S(2)}) collective-permute-start(bf16[8,1040,256]{2,1,0:T(8,128)(2,1)} %all-to-all-done.k_ref.v_ref.rate_ref), channel_id=1, source_target_pairs={{0,8},{8,16},{16,24},{1,9},{9,17},{17,25},{2,10},{10,18},{18,26},{... | collective-permute-start | bytes 12779528 | tf_op jit(solution)/shard_map/ppermute | solution.py:37
  249.6 52.1 %all-to-all-start.2 = ((bf16[8,512,256]{2,1,0:T(8,128)(2,1)}), bf16[8,512,256]{2,1,0:T(8,128)(2,1)}, u32[]{:S(2)}, u32[]{:S(2)}) async-start(bf16[8,512,256]{2,1,0:T(8,128)(2,1)} %shard_map.66), calls=%async_computation.2 | async-start | bytes 4194304 | tf_op jit(solution)/shard_map/all_to_all | solution.py:41
  258.4 52.0 %collective-permute-start.4 = (bf16[8,1024,256]{2,1,0:T(8,128)(2,1)}, bf16[8,1024,256]{2,1,0:T(8,128)(2,1)}, u32[]{:S(2)}, u32[]{:S(2)}) collective-permute-start(bf16[8,1024,256]{2,1,0:T(8,128)(2,1)} %slice.10.k_ref.v_ref), channel_id=1, source_target_pairs={{0,8},{8,16},{16,24},{1,9},{9,17},{17,25},{2,10},{10,18},{18,26},{... | collective-permute-start | bytes 12582920 | tf_op jit(solution)/shard_map/ppermute | solution.py:37
  271.1 34.9 %collective-permute-start.5 = (bf16[3,2,256,256]{3,2,1,0:T(8,128)(2,1)S(1)}, bf16[3,2,256,256]{3,2,1,0:T(8,128)(2,1)S(1)}, u32[]{:S(2)}, u32[]{:S(2)}) collective-permute-start(bf16[3,2,256,256]{3,2,1,0:T(8,128)(2,1)S(1)} %convert_element_type.33), channel_id=1, source_target_pairs={{0,8},{1,9},{2,10},{3,11},{4,12},{5,13},{6,14},{7,15}} | collective-permute-start | bytes 2359304 | tf_op jit(solution)/shard_map/ppermute | solution.py:317
  295.1 10.9 %copy-start.2 = (f32[3,2,256,256]{3,2,1,0:T(8,128)S(1)}, f32[3,2,256,256]{3,2,1,0:T(8,128)}, u32[]{:S(2)}) copy-start(f32[3,2,256,256]{3,2,1,0:T(8,128)} %shard_map.68) | copy-start | bytes 4718596
  301.7 97.1 %all-to-all-start.3 = ((bf16[8,2,256,256]{3,2,1,0:T(8,128)(2,1)}), bf16[8,2,256,256]{3,2,1,0:T(8,128)(2,1)}, u32[]{:S(2)}, u32[]{:S(2)}) async-start(bf16[8,2,256,256]{3,2,1,0:T(8,128)(2,1)} %shard_map.69), calls=%async_computation.3 | async-start | bytes 4194304 | tf_op jit(solution)/shard_map/all_to_all | solution.py:41
  306.2 2.2 copy-start.1
  306.3 0.9 collective-permute-start.6
  307.4 1.0 collective-permute-start.7
  331.6 10.0 %collective-permute-start.8 = (bf16[2,256,256]{2,1,0:T(8,128)(2,1)}, bf16[2,256,256]{2,1,0:T(8,128)(2,1)S(1)}, u32[]{:S(2)}, u32[]{:S(2)}) collective-permute-start(bf16[2,256,256]{2,1,0:T(8,128)(2,1)} %get-tuple-element.27), channel_id=1, source_target_pairs={{0,1},{1,0},{2,3},{3,2},{4,5},{5,4},{6,7},{7,6},{8,9},{9,8},{10,11... | collective-permute-start | bytes 786440 | tf_op jit(solution)/shard_map/ppermute | solution.py:267
  333.5 9.3 %collective-permute-start.9 = (bf16[2,256,256]{2,1,0:T(8,128)(2,1)}, bf16[2,256,256]{2,1,0:T(8,128)(2,1)S(1)}, u32[]{:S(2)}, u32[]{:S(2)}) collective-permute-start(bf16[2,256,256]{2,1,0:T(8,128)(2,1)} %get-tuple-element.28), channel_id=1, source_target_pairs={{0,2},{1,3},{2,0},{3,1},{4,6},{5,7},{6,4},{7,5},{8,10},{9,11},{10,... | collective-permute-start | bytes 786440 | tf_op jit(solution)/shard_map/ppermute | solution.py:267
  335.0 15.4 %collective-permute-start.10 = (bf16[2,256,256]{2,1,0:T(8,128)(2,1)}, bf16[2,256,256]{2,1,0:T(8,128)(2,1)S(1)}, u32[]{:S(2)}, u32[]{:S(2)}) collective-permute-start(bf16[2,256,256]{2,1,0:T(8,128)(2,1)} %get-tuple-element.29), channel_id=1, source_target_pairs={{0,7},{1,6},{2,5},{3,4},{4,3},{5,2},{6,1},{7,0},{8,15},{9,14},{10,... | collective-permute-start | bytes 786440 | tf_op jit(solution)/shard_map/ppermute | solution.py:267
  337.4 16.9 %collective-permute-start.11 = (bf16[2,256,256]{2,1,0:T(8,128)(2,1)}, bf16[2,256,256]{2,1,0:T(8,128)(2,1)S(1)}, u32[]{:S(2)}, u32[]{:S(2)}) collective-permute-start(bf16[2,256,256]{2,1,0:T(8,128)(2,1)} %get-tuple-element.30), channel_id=1, source_target_pairs={{0,6},{1,7},{2,4},{3,5},{4,2},{5,3},{6,0},{7,1},{8,14},{9,15},{10,... | collective-permute-start | bytes 786440 | tf_op jit(solution)/shard_map/ppermute | solution.py:267
  338.8 56.2 %collective-permute-start.12 = (bf16[2,256,256]{2,1,0:T(8,128)(2,1)}, bf16[2,256,256]{2,1,0:T(8,128)(2,1)S(1)}, u32[]{:S(2)}, u32[]{:S(2)}) collective-permute-start(bf16[2,256,256]{2,1,0:T(8,128)(2,1)} %get-tuple-element.31), channel_id=1, source_target_pairs={{0,5},{1,4},{2,7},{3,6},{4,1},{5,0},{6,3},{7,2},{8,13},{9,12},{10,... | collective-permute-start | bytes 786440 | tf_op jit(solution)/shard_map/ppermute | solution.py:267
  341.6 57.1 %copy-start.4 = (bf16[2,256,256]{2,1,0:T(8,128)(2,1)}, bf16[2,256,256]{2,1,0:T(8,128)(2,1)S(1)}, u32[]{:S(2)}) copy-start(bf16[2,256,256]{2,1,0:T(8,128)(2,1)S(1)} %collective-permute-done.8.refs_0_) | copy-start | bytes 786436
  341.6 57.1 %collective-permute-start.13 = (bf16[2,256,256]{2,1,0:T(8,128)(2,1)}, bf16[2,256,256]{2,1,0:T(8,128)(2,1)S(1)}, u32[]{:S(2)}, u32[]{:S(2)}) collective-permute-start(bf16[2,256,256]{2,1,0:T(8,128)(2,1)} %get-tuple-element.32), channel_id=1, source_target_pairs={{0,4},{1,5},{2,6},{3,7},{4,0},{5,1},{6,2},{7,3},{8,12},{9,13},{10,... | collective-permute-start | bytes 786440 | tf_op jit(solution)/shard_map/ppermute | solution.py:267
  342.9 55.9 %copy-start.5 = (bf16[2,256,256]{2,1,0:T(8,128)(2,1)}, bf16[2,256,256]{2,1,0:T(8,128)(2,1)S(1)}, u32[]{:S(2)}) copy-start(bf16[2,256,256]{2,1,0:T(8,128)(2,1)S(1)} %collective-permute-done.9.refs_1_) | copy-start | bytes 786436
  342.9 55.8 %collective-permute-start.14 = (bf16[2,256,256]{2,1,0:T(8,128)(2,1)}, bf16[2,256,256]{2,1,0:T(8,128)(2,1)S(1)}, u32[]{:S(2)}, u32[]{:S(2)}) collective-permute-start(bf16[2,256,256]{2,1,0:T(8,128)(2,1)} %get-tuple-element.33), channel_id=1, source_target_pairs={{0,3},{1,2},{2,1},{3,0},{4,7},{5,6},{6,5},{7,4},{8,11},{9,10},{10,... | collective-permute-start | bytes 786440 | tf_op jit(solution)/shard_map/ppermute | solution.py:267
  350.4 48.3 %copy-start.6 = (bf16[2,256,256]{2,1,0:T(8,128)(2,1)}, bf16[2,256,256]{2,1,0:T(8,128)(2,1)S(1)}, u32[]{:S(2)}) copy-start(bf16[2,256,256]{2,1,0:T(8,128)(2,1)S(1)} %collective-permute-done.10.refs_2_) | copy-start | bytes 786436
  354.3 44.5 %copy-start.7 = (bf16[2,256,256]{2,1,0:T(8,128)(2,1)}, bf16[2,256,256]{2,1,0:T(8,128)(2,1)S(1)}, u32[]{:S(2)}) copy-start(bf16[2,256,256]{2,1,0:T(8,128)(2,1)S(1)} %collective-permute-done.11.refs_3_) | copy-start | bytes 786436
  395.0 3.8 copy-start.8
  398.7 0.7 copy-start.9
  398.7 0.8 copy-start.10

commit v4 on v3

--- a/solution.py
+++ b/solution.py
@@ -202,10 +202,8 @@
         top_far = jnp.max(far, axis=1, keepdims=True)
         top_near = jnp.max(near, axis=1, keepdims=True)
         top = jnp.where(first, top_near, jnp.maximum(top_near, top_far))
-        shift = top * factor
-        shift_far = jnp.where(first, jnp.inf, shift)
-        w_far = jnp.exp2(far * factor - shift_far)
-        w_near = jnp.exp2(near * factor - shift)
+        w_far = jnp.exp2((far - jnp.where(first, jnp.inf, top)) * factor)
+        w_near = jnp.exp2((near - top) * factor)
         weight = jnp.sum(w_far, axis=1, keepdims=True) + jnp.sum(w_near, axis=1, keepdims=True)
         attended = dot(w_far.astype(jnp.bfloat16), flat(ev_ref, start, length))
         attended += dot(w_near.astype(jnp.bfloat16), flat(v_ref, 0, stop))

time: 405 us -> 405 us (level)
  transfers between devices with their start and end apart: 19 -> 19, of which waited for: 10 -> 10; matrix products, arithmetic and copies ran while one was open for 4% -> 4% of each run, Pallas kernels for 17% -> 16%
where the time goes in v4:
time: 405 us; the launch traced here: 404 us
  waiting for transfers between devices  242 us (60%)
  Pallas kernels  76.8 us (19%)
  starting transfers between devices  67.5 us (17%)
  other arithmetic  12.5 us (3%)
  local copies, waits for them, and re-layouts  5.25 us (1%)
    all_to_all x4, waiting for transfers between devices, exchange(): lax.all_to_all(value, 'head', split_axis=0, concat_axis=0, tiled=True)  185 us
    ppermute x7, waiting for transfers between devices, swap(): lax.ppermute(pieces[step], 'head', [(i, i ^ step) for i in range(count)])  54.2 us
    pallas_call x2, Pallas kernels, attend(): pl.pallas_call(attend_kernel, grid=(group,), in_specs=[pl.BlockSpec(memor...  42.1 us
    ppermute x2, starting transfers between devices, from_behind(): lax.ppermute(value, axis, [(source, source + steps) for source in range(c...  25.5 us
    all_to_all x4, starting transfers between devices, exchange(): lax.all_to_all(value, 'head', split_axis=0, concat_axis=0, tiled=True)  20.7 us
    pallas_call x2, Pallas kernels, updates(): pl.pallas_call(functools.partial(update_kernel, first_head), grid=(group,...  15.8 us
    pallas_call x3, Pallas kernels, pack(): pl.pallas_call(body, in_specs=specs, out_specs=pl.BlockSpec(memory_space=...  14.2 us
    ppermute x7, starting transfers between devices, swap(): lax.ppermute(pieces[step], 'head', [(i, i ^ step) for i in range(count)])  13 us
  transfers between devices with their start and end apart: 19, of which 10 were waited for; matrix products, arithmetic and copies ran while one was open for 4% of the time, Pallas kernels for 16%

profile of v4, /device:TPU:0, one launch (start us, length us, event | category | flops | bytes accessed | tf_op | source)
XLA Modules:
  0.0 404.2 jit_solution(5732116534599954534)
XLA Ops:
  0.0 5.5 %shard_map.64 = bf16[8,1040,256]{2,1,0:T(8,128)(2,1)} custom-call(bf16[32,256]{1,0:T(8,128)(2,1)} %bitcast.5, bf16[256,8192]{1,0:T(8,128)(2,1)} %refs_0_.4, bf16[256,8192]{1,0:T(8,128)(2,1)} %refs_1_.3), custom_call_target="tpu_custom_call" | custom-call | bytes 8519 | tf_op jit(solution)/shard_map/pallas_call | solution.py:113
  5.5 7.3 %all-to-all-start = ((bf16[8,1040,256]{2,1,0:T(8,128)(2,1)}), bf16[8,1040,256]{2,1,0:T(8,128)(2,1)}, u32[]{:S(2)}, u32[]{:S(2)}) async-start(bf16[8,1040,256]{2,1,0:T(8,128)(2,1)} %shard_map.64), calls=%async_computation | async-start | bytes 8519680 | tf_op jit(solution)/shard_map/all_to_all | solution.py:41
  12.8 6.0 %shard_map.65 = bf16[8,1536,256]{2,1,0:T(8,128)(2,1)} custom-call(bf16[256,8192]{1,0:T(8,128)(2,1)} %refs_0_.4, bf16[256,8192]{1,0:T(8,128)(2,1)} %refs_1_.3, bf16[256,8192]{1,0:T(8,128)(2,1)} %refs_0_.5), custom_call_target="tpu_custom_call" | custom-call | bytes 12582 | tf_op jit(solution)/shard_map/pallas_call | solution.py:113
  18.8 88.7 %all-to-all-done.k_ref.v_ref.rate_ref = bf16[8,1040,256]{2,1,0:T(8,128)(2,1)} async-done(((bf16[8,1040,256]{2,1,0:T(8,128)(2,1)}), bf16[8,1040,256]{2,1,0:T(8,128)(2,1)}, u32[]{:S(2)}, u32[]{:S(2)}) %all-to-all-start) | async-done | bytes 4259872 | tf_op jit(solution)/shard_map/all_to_all | solution.py:41
  107.5 4.8 %all-to-all-start.1 = ((bf16[8,1536,256]{2,1,0:T(8,128)(2,1)}), bf16[8,1536,256]{2,1,0:T(8,128)(2,1)}, u32[]{:S(2)}, u32[]{:S(2)}) async-start(bf16[8,1536,256]{2,1,0:T(8,128)(2,1)} %shard_map.65), calls=%async_computation.1 | async-start | bytes 12582912 | tf_op jit(solution)/shard_map/all_to_all | solution.py:41
  112.3 7.9 %shard_map.67 = f32[3,2,256,256]{3,2,1,0:T(8,128)} custom-call(bf16[8,1040,256]{2,1,0:T(8,128)(2,1)} %all-to-all-done.k_ref.v_ref.rate_ref, bf16[8,1040,256]{2,1,0:T(8,128)(2,1)} %all-to-all-done.k_ref.v_ref.rate_ref, bf16[8,1040,256]{2,1,0:T(8,128)(2,1)} %all-to-all-done.k_ref.v_ref.rate_ref, bf16[3,4,256,256]{3,2,1,0:T(8,128)(2,1)} %init_ref.3), custom_call_target="tpu_custom_call" | custom-call | flops 3221225 | bytes 4194 | tf_op jit(solution)/shard_map/pallas_call | solution.py:162
  120.2 1.5 collective-permute-start
  121.7 3.1 collective-permute-done
  124.8 1.6 add.46
  128.7 1.9 collective-permute-start.2
  130.6 2.7 shard_map.66
  133.3 22.1 %collective-permute-start.3 = (bf16[8,1040,256]{2,1,0:T(8,128)(2,1)}, bf16[8,1040,256]{2,1,0:T(8,128)(2,1)}, u32[]{:S(2)}, u32[]{:S(2)}) collective-permute-start(bf16[8,1040,256]{2,1,0:T(8,128)(2,1)} %all-to-all-done.k_ref.v_ref.rate_ref), channel_id=1, source_target_pairs={{0,8},{8,16},{16,24},{1,9},{9,17},{17,25},{2,10},{10,18},{18,26},{... | collective-permute-start | bytes 12779528 | tf_op jit(solution)/shard_map/ppermute | solution.py:37
  155.5 2.1 fusion.1
  157.6 2.8 multiply_convert_fusion.1.fit_ref
  160.4 89.2 %all-to-all-done.1.q_ref = bf16[8,1536,256]{2,1,0:T(8,128)(2,1)} async-done(((bf16[8,1536,256]{2,1,0:T(8,128)(2,1)}), bf16[8,1536,256]{2,1,0:T(8,128)(2,1)}, u32[]{:S(2)}, u32[]{:S(2)}) %all-to-all-start.1) | async-done | bytes 6291488 | tf_op jit(solution)/shard_map/all_to_all | solution.py:41
  249.6 4.3 %all-to-all-start.2 = ((bf16[8,512,256]{2,1,0:T(8,128)(2,1)}), bf16[8,512,256]{2,1,0:T(8,128)(2,1)}, u32[]{:S(2)}, u32[]{:S(2)}) async-start(bf16[8,512,256]{2,1,0:T(8,128)(2,1)} %shard_map.66), calls=%async_computation.2 | async-start | bytes 4194304 | tf_op jit(solution)/shard_map/all_to_all | solution.py:41
  253.9 4.5 %slice.10.k_ref.v_ref = bf16[8,1024,256]{2,1,0:T(8,128)(2,1)} slice(bf16[8,1536,256]{2,1,0:T(8,128)(2,1)} %all-to-all-done.1.q_ref), slice={[0:8], [0:1024], [0:256]} | slice | bytes 8388608 | tf_op jit(solution)/shard_map/slice | solution.py:345
  258.4 3.4 collective-permute-start.4
  261.7 7.9 %shard_map.68 = f32[3,2,256,256]{3,2,1,0:T(8,128)} custom-call(bf16[8,1024,256]{2,1,0:T(8,128)(2,1)} %slice.10.k_ref.v_ref, bf16[8,1024,256]{2,1,0:T(8,128)(2,1)} %slice.10.k_ref.v_ref, bf16[8,1040,256]{2,1,0:T(8,128)(2,1)} %all-to-all-done.k_ref.v_ref.rate_ref, bf16[3,4,256,256]{3,2,1,0:T(8,128)(2,1)} %init_ref.3), custom_call_target="tpu_custom_call" | custom-call | flops 3221225 | bytes 4194 | tf_op jit(solution)/shard_map/pallas_call | solution.py:162
  271.1 2.3 collective-permute-start.5
  274.0 21.0 %shard_map.69 = bf16[8,2,256,256]{3,2,1,0:T(8,128)(2,1)} custom-call(s32[2]{0:T(128)} %pad_add_fusion.place_ref, bf16[8,1536,256]{2,1,0:T(8,128)(2,1)} %all-to-all-done.1.q_ref, bf16[8,1040,256]{2,1,0:T(8,128)(2,1)} %all-to-all-done.k_ref.v_ref.rate_ref, bf16[8,1040,256]{2,1,0:T(8,128)(2,1)} %all-to-all-done.k_ref.v_ref.rate_ref, ...), custom_call_target="tpu_custom_call" | custom-call | flops 11274289 | bytes 12582 | tf_op jit(solution)/shard_map/pallas_call | solution.py:229
  295.0 6.6 %all-to-all-done.2.q_ref = bf16[8,512,256]{2,1,0:T(8,128)(2,1)} async-done(((bf16[8,512,256]{2,1,0:T(8,128)(2,1)}), bf16[8,512,256]{2,1,0:T(8,128)(2,1)}, u32[]{:S(2)}, u32[]{:S(2)}) %all-to-all-start.2) | async-done | bytes 2097184 | tf_op jit(solution)/shard_map/all_to_all | solution.py:41
  301.7 4.3 %all-to-all-start.3 = ((bf16[8,2,256,256]{3,2,1,0:T(8,128)(2,1)}), bf16[8,2,256,256]{3,2,1,0:T(8,128)(2,1)}, u32[]{:S(2)}, u32[]{:S(2)}) async-start(bf16[8,2,256,256]{3,2,1,0:T(8,128)(2,1)} %shard_map.69), calls=%async_computation.3 | async-start | bytes 4194304 | tf_op jit(solution)/shard_map/all_to_all | solution.py:41
  310.4 21.1 %shard_map.70 = (bf16[2,256,256]{2,1,0:T(8,128)(2,1)}, bf16[2,256,256]{2,1,0:T(8,128)(2,1)}, bf16[2,256,256]{2,1,0:T(8,128)(2,1)}, bf16[2,256,256]{2,1,0:T(8,128...) custom-call(s32[2]{0:T(128)} %pad_add_fusion.place_ref, ...), custom_call_target="tpu_custom_call" | custom-call | flops 11274289 | bytes 12582 | tf_op jit(solution)/shard_map/pallas_call | solution.py:229
  331.5 1.9 collective-permute-start.8
  335.0 2.4 collective-permute-start.10
  342.9 3.2 collective-permute-start.14
  346.1 4.4 %collective-permute-done.10.refs_2_ = bf16[2,256,256]{2,1,0:T(8,128)(2,1)S(1)} collective-permute-done((bf16[2,256,256]{2,1,0:T(8,128)(2,1)}, bf16[2,256,256]{2,1,0:T(8,128)(2,1)S(1)}, u32[]{:S(2)}, u32[]{:S(2)}) %collective-permute-start.10) | collective-permute-done | bytes 262176 | tf_op jit(solution)/shard_map/ppermute | solution.py:265
  350.5 3.9 collective-permute-done.11.refs_3_
  354.4 40.6 %collective-permute-done.12.refs_4_ = bf16[2,256,256]{2,1,0:T(8,128)(2,1)S(1)} collective-permute-done((bf16[2,256,256]{2,1,0:T(8,128)(2,1)}, bf16[2,256,256]{2,1,0:T(8,128)(2,1)S(1)}, u32[]{:S(2)}, u32[]{:S(2)}) %collective-permute-start.12) | collective-permute-done | bytes 262176 | tf_op jit(solution)/shard_map/ppermute | solution.py:265
  395.0 3.7 collective-permute-done.13.refs_5_
  399.5 4.6 %shard_map.71 = bf16[256,8192]{1,0:T(8,128)(2,1)} custom-call(s32[2]{0:T(128)} %pad_add_fusion.place_ref, bf16[8,2,256,256]{3,2,1,0:T(8,128)(2,1)} %all-to-all-done.3.first_ref, bf16[2,256,256]{2,1,0:T(8,128)(2,1)} %copy-done.4, bf16[2,256,256]{2,1,0:T(8,128)(2,1)} %copy-done.5, bf16[2,256,256]{2,1,0:T(8,128)(2,1)} %copy-done.6, ...), custom_call_target="tpu_custom_call" | custom-call | flops 10485 | bytes 8388 | tf_op jit(solution)/shard_map/pallas_call | solution.py:295
  (50 shorter events, 16.4 us)
Async XLA Ops:
  5.5 102.0 %all-to-all-start = ((bf16[8,1040,256]{2,1,0:T(8,128)(2,1)}), bf16[8,1040,256]{2,1,0:T(8,128)(2,1)}, u32[]{:S(2)}, u32[]{:S(2)}) async-start(bf16[8,1040,256]{2,1,0:T(8,128)(2,1)} %shard_map.64), calls=%async_computation | async-start | bytes 8519680 | tf_op jit(solution)/shard_map/all_to_all | solution.py:41
  107.5 142.0 %all-to-all-start.1 = ((bf16[8,1536,256]{2,1,0:T(8,128)(2,1)}), bf16[8,1536,256]{2,1,0:T(8,128)(2,1)}, u32[]{:S(2)}, u32[]{:S(2)}) async-start(bf16[8,1536,256]{2,1,0:T(8,128)(2,1)} %shard_map.65), calls=%async_computation.1 | async-start | bytes 12582912 | tf_op jit(solution)/shard_map/all_to_all | solution.py:41
  120.2 7.0 %copy-start.3 = (f32[3,2,256,256]{3,2,1,0:T(8,128)S(1)}, f32[3,2,256,256]{3,2,1,0:T(8,128)}, u32[]{:S(2)}) copy-start(f32[3,2,256,256]{3,2,1,0:T(8,128)} %shard_map.67) | copy-start | bytes 4718596
  120.2 4.6 %collective-permute-start = (f32[3,2,256,256]{3,2,1,0:T(8,128)}, f32[3,2,256,256]{3,2,1,0:T(8,128)S(1)}, u32[]{:S(2)}, u32[]{:S(2)}) collective-permute-start(f32[3,2,256,256]{3,2,1,0:T(8,128)} %shard_map.67), channel_id=1, source_target_pairs={{0,8},{1,9},{2,10},{3,11},{4,12},{5,13},{6,14},{7,15}} | collective-permute-start | bytes 4718600 | tf_op jit(solution)/shard_map/ppermute | solution.py:315
  126.4 0.8 collective-permute-start.1
  128.7 26.8 %copy-start = (bf16[3,4,256,256]{3,2,1,0:T(8,128)(2,1)S(1)}, bf16[3,4,256,256]{3,2,1,0:T(8,128)(2,1)}, u32[]{:S(2)}) copy-start(bf16[3,4,256,256]{3,2,1,0:T(8,128)(2,1)} %init_ref.3) | copy-start | bytes 4718596
  128.7 26.8 %collective-permute-start.2 = (f32[3,2,256,256]{3,2,1,0:T(8,128)}, f32[3,2,256,256]{3,2,1,0:T(8,128)}, u32[]{:S(2)}, u32[]{:S(2)}) collective-permute-start(f32[3,2,256,256]{3,2,1,0:T(8,128)} %get-tuple-element.38), channel_id=1, source_target_pairs={{16,24},{17,25},{18,26},{19,27},{20,28},{21,29},{22,30},{23,31}} | collective-permute-start | bytes 4718600 | tf_op jit(solution)/shard_map/ppermute | solution.py:315
  133.3 140.7 %collective-permute-start.3 = (bf16[8,1040,256]{2,1,0:T(8,128)(2,1)}, bf16[8,1040,256]{2,1,0:T(8,128)(2,1)}, u32[]{:S(2)}, u32[]{:S(2)}) collective-permute-start(bf16[8,1040,256]{2,1,0:T(8,128)(2,1)} %all-to-all-done.k_ref.v_ref.rate_ref), channel_id=1, source_target_pairs={{0,8},{8,16},{16,24},{1,9},{9,17},{17,25},{2,10},{10,18},{18,26},{... | collective-permute-start | bytes 12779528 | tf_op jit(solution)/shard_map/ppermute | solution.py:37
  249.6 52.1 %all-to-all-start.2 = ((bf16[8,512,256]{2,1,0:T(8,128)(2,1)}), bf16[8,512,256]{2,1,0:T(8,128)(2,1)}, u32[]{:S(2)}, u32[]{:S(2)}) async-start(bf16[8,512,256]{2,1,0:T(8,128)(2,1)} %shard_map.66), calls=%async_computation.2 | async-start | bytes 4194304 | tf_op jit(solution)/shard_map/all_to_all | solution.py:41
  258.4 52.0 %collective-permute-start.4 = (bf16[8,1024,256]{2,1,0:T(8,128)(2,1)}, bf16[8,1024,256]{2,1,0:T(8,128)(2,1)}, u32[]{:S(2)}, u32[]{:S(2)}) collective-permute-start(bf16[8,1024,256]{2,1,0:T(8,128)(2,1)} %slice.10.k_ref.v_ref), channel_id=1, source_target_pairs={{0,8},{8,16},{16,24},{1,9},{9,17},{17,25},{2,10},{10,18},{18,26},{... | collective-permute-start | bytes 12582920 | tf_op jit(solution)/shard_map/ppermute | solution.py:37
  271.1 34.9 %collective-permute-start.5 = (bf16[3,2,256,256]{3,2,1,0:T(8,128)(2,1)S(1)}, bf16[3,2,256,256]{3,2,1,0:T(8,128)(2,1)S(1)}, u32[]{:S(2)}, u32[]{:S(2)}) collective-permute-start(bf16[3,2,256,256]{3,2,1,0:T(8,128)(2,1)S(1)} %convert_element_type.33), channel_id=1, source_target_pairs={{0,8},{1,9},{2,10},{3,11},{4,12},{5,13},{6,14},{7,15}} | collective-permute-start | bytes 2359304 | tf_op jit(solution)/shard_map/ppermute | solution.py:315
  295.0 11.0 %copy-start.2 = (f32[3,2,256,256]{3,2,1,0:T(8,128)S(1)}, f32[3,2,256,256]{3,2,1,0:T(8,128)}, u32[]{:S(2)}) copy-start(f32[3,2,256,256]{3,2,1,0:T(8,128)} %shard_map.68) | copy-start | bytes 4718596
  301.7 97.1 %all-to-all-start.3 = ((bf16[8,2,256,256]{3,2,1,0:T(8,128)(2,1)}), bf16[8,2,256,256]{3,2,1,0:T(8,128)(2,1)}, u32[]{:S(2)}, u32[]{:S(2)}) async-start(bf16[8,2,256,256]{3,2,1,0:T(8,128)(2,1)} %shard_map.69), calls=%async_computation.3 | async-start | bytes 4194304 | tf_op jit(solution)/shard_map/all_to_all | solution.py:41
  306.2 2.2 copy-start.1
  306.3 0.9 collective-permute-start.6
  307.4 1.0 collective-permute-start.7
  331.5 10.1 %collective-permute-start.8 = (bf16[2,256,256]{2,1,0:T(8,128)(2,1)}, bf16[2,256,256]{2,1,0:T(8,128)(2,1)S(1)}, u32[]{:S(2)}, u32[]{:S(2)}) collective-permute-start(bf16[2,256,256]{2,1,0:T(8,128)(2,1)} %get-tuple-element.27), channel_id=1, source_target_pairs={{0,1},{1,0},{2,3},{3,2},{4,5},{5,4},{6,7},{7,6},{8,9},{9,8},{10,11... | collective-permute-start | bytes 786440 | tf_op jit(solution)/shard_map/ppermute | solution.py:265
  333.5 9.4 %collective-permute-start.9 = (bf16[2,256,256]{2,1,0:T(8,128)(2,1)}, bf16[2,256,256]{2,1,0:T(8,128)(2,1)S(1)}, u32[]{:S(2)}, u32[]{:S(2)}) collective-permute-start(bf16[2,256,256]{2,1,0:T(8,128)(2,1)} %get-tuple-element.28), channel_id=1, source_target_pairs={{0,2},{1,3},{2,0},{3,1},{4,6},{5,7},{6,4},{7,5},{8,10},{9,11},{10,... | collective-permute-start | bytes 786440 | tf_op jit(solution)/shard_map/ppermute | solution.py:265
  335.0 15.5 %collective-permute-start.10 = (bf16[2,256,256]{2,1,0:T(8,128)(2,1)}, bf16[2,256,256]{2,1,0:T(8,128)(2,1)S(1)}, u32[]{:S(2)}, u32[]{:S(2)}) collective-permute-start(bf16[2,256,256]{2,1,0:T(8,128)(2,1)} %get-tuple-element.29), channel_id=1, source_target_pairs={{0,7},{1,6},{2,5},{3,4},{4,3},{5,2},{6,1},{7,0},{8,15},{9,14},{10,... | collective-permute-start | bytes 786440 | tf_op jit(solution)/shard_map/ppermute | solution.py:265
  337.3 17.1 %collective-permute-start.11 = (bf16[2,256,256]{2,1,0:T(8,128)(2,1)}, bf16[2,256,256]{2,1,0:T(8,128)(2,1)S(1)}, u32[]{:S(2)}, u32[]{:S(2)}) collective-permute-start(bf16[2,256,256]{2,1,0:T(8,128)(2,1)} %get-tuple-element.30), channel_id=1, source_target_pairs={{0,6},{1,7},{2,4},{3,5},{4,2},{5,3},{6,0},{7,1},{8,14},{9,15},{10,... | collective-permute-start | bytes 786440 | tf_op jit(solution)/shard_map/ppermute | solution.py:265
  338.8 56.2 %collective-permute-start.12 = (bf16[2,256,256]{2,1,0:T(8,128)(2,1)}, bf16[2,256,256]{2,1,0:T(8,128)(2,1)S(1)}, u32[]{:S(2)}, u32[]{:S(2)}) collective-permute-start(bf16[2,256,256]{2,1,0:T(8,128)(2,1)} %get-tuple-element.31), channel_id=1, source_target_pairs={{0,5},{1,4},{2,7},{3,6},{4,1},{5,0},{6,3},{7,2},{8,13},{9,12},{10,... | collective-permute-start | bytes 786440 | tf_op jit(solution)/shard_map/ppermute | solution.py:265
  341.6 57.1 %copy-start.4 = (bf16[2,256,256]{2,1,0:T(8,128)(2,1)}, bf16[2,256,256]{2,1,0:T(8,128)(2,1)S(1)}, u32[]{:S(2)}) copy-start(bf16[2,256,256]{2,1,0:T(8,128)(2,1)S(1)} %collective-permute-done.8.refs_0_) | copy-start | bytes 786436
  341.6 57.1 %collective-permute-start.13 = (bf16[2,256,256]{2,1,0:T(8,128)(2,1)}, bf16[2,256,256]{2,1,0:T(8,128)(2,1)S(1)}, u32[]{:S(2)}, u32[]{:S(2)}) collective-permute-start(bf16[2,256,256]{2,1,0:T(8,128)(2,1)} %get-tuple-element.32), channel_id=1, source_target_pairs={{0,4},{1,5},{2,6},{3,7},{4,0},{5,1},{6,2},{7,3},{8,12},{9,13},{10,... | collective-permute-start | bytes 786440 | tf_op jit(solution)/shard_map/ppermute | solution.py:265
  342.9 55.9 %copy-start.5 = (bf16[2,256,256]{2,1,0:T(8,128)(2,1)}, bf16[2,256,256]{2,1,0:T(8,128)(2,1)S(1)}, u32[]{:S(2)}) copy-start(bf16[2,256,256]{2,1,0:T(8,128)(2,1)S(1)} %collective-permute-done.9.refs_1_) | copy-start | bytes 786436
  342.9 55.8 %collective-permute-start.14 = (bf16[2,256,256]{2,1,0:T(8,128)(2,1)}, bf16[2,256,256]{2,1,0:T(8,128)(2,1)S(1)}, u32[]{:S(2)}, u32[]{:S(2)}) collective-permute-start(bf16[2,256,256]{2,1,0:T(8,128)(2,1)} %get-tuple-element.33), channel_id=1, source_target_pairs={{0,3},{1,2},{2,1},{3,0},{4,7},{5,6},{6,5},{7,4},{8,11},{9,10},{10,... | collective-permute-start | bytes 786440 | tf_op jit(solution)/shard_map/ppermute | solution.py:265
  350.5 48.3 %copy-start.6 = (bf16[2,256,256]{2,1,0:T(8,128)(2,1)}, bf16[2,256,256]{2,1,0:T(8,128)(2,1)S(1)}, u32[]{:S(2)}) copy-start(bf16[2,256,256]{2,1,0:T(8,128)(2,1)S(1)} %collective-permute-done.10.refs_2_) | copy-start | bytes 786436
  354.4 44.4 %copy-start.7 = (bf16[2,256,256]{2,1,0:T(8,128)(2,1)}, bf16[2,256,256]{2,1,0:T(8,128)(2,1)S(1)}, u32[]{:S(2)}) copy-start(bf16[2,256,256]{2,1,0:T(8,128)(2,1)S(1)} %collective-permute-done.11.refs_3_) | copy-start | bytes 786436
  395.0 3.8 copy-start.8
  398.7 0.7 copy-start.9
  398.7 0.8 copy-start.10

commit v5 on v4

--- a/solution.py
+++ b/solution.py
@@ -255,8 +255,8 @@
 
 
 def swap_order(count):
-    short = [step for step in (1, 2) if step < count]
-    return short + list(range(count - 1, 2, -1)) + [0]
+    short = [step for step in (2, 3) if step < count]
+    return short + list(range(count - 1, 3, -1)) + [1, 0]
 
 
 def swap(pieces):

time: 405 us -> 405 us (level)
  transfers between devices with their start and end apart: 19 -> 19, of which waited for: 10 -> 9; matrix products, arithmetic and copies ran while one was open for 4% -> 4% of each run, Pallas kernels for 16% -> 16%
where the time goes in v5:
time: 405 us; the launch traced here: 404 us
  waiting for transfers between devices  240 us (59%)
  Pallas kernels  76.7 us (19%)
  starting transfers between devices  69.3 us (17%)
  other arithmetic  12.5 us (3%)
  local copies, waits for them, and re-layouts  5.25 us (1%)
    all_to_all x4, waiting for transfers between devices, exchange(): lax.all_to_all(value, 'head', split_axis=0, concat_axis=0, tiled=True)  185 us
    ppermute x7, waiting for transfers between devices, swap(): lax.ppermute(pieces[step], 'head', [(i, i ^ step) for i in range(count)])  52.5 us
    pallas_call x2, Pallas kernels, attend(): pl.pallas_call(attend_kernel, grid=(group,), in_specs=[pl.BlockSpec(memor...  42.1 us
    ppermute x2, starting transfers between devices, from_behind(): lax.ppermute(value, axis, [(source, source + steps) for source in range(c...  25.5 us
    all_to_all x4, starting transfers between devices, exchange(): lax.all_to_all(value, 'head', split_axis=0, concat_axis=0, tiled=True)  20.7 us
    pallas_call x2, Pallas kernels, updates(): pl.pallas_call(functools.partial(update_kernel, first_head), grid=(group,...  15.8 us
    ppermute x7, starting transfers between devices, swap(): lax.ppermute(pieces[step], 'head', [(i, i ^ step) for i in range(count)])  14.7 us
    pallas_call x3, Pallas kernels, pack(): pl.pallas_call(body, in_specs=specs, out_specs=pl.BlockSpec(memory_space=...  14.2 us
  transfers between devices with their start and end apart: 19, of which 9 were waited for; matrix products, arithmetic and copies ran while one was open for 4% of the time, Pallas kernels for 16%

profile of v5, /device:TPU:0, one launch (start us, length us, event | category | flops | bytes accessed | tf_op | source)
XLA Modules:
  0.0 404.2 jit_solution(8001724301857124510)
XLA Ops:
  0.0 5.5 %shard_map.64 = bf16[8,1040,256]{2,1,0:T(8,128)(2,1)} custom-call(bf16[32,256]{1,0:T(8,128)(2,1)} %bitcast.5, bf16[256,8192]{1,0:T(8,128)(2,1)} %refs_0_.4, bf16[256,8192]{1,0:T(8,128)(2,1)} %refs_1_.3), custom_call_target="tpu_custom_call" | custom-call | bytes 8519 | tf_op jit(solution)/shard_map/pallas_call | solution.py:113
  5.5 7.3 %all-to-all-start = ((bf16[8,1040,256]{2,1,0:T(8,128)(2,1)}), bf16[8,1040,256]{2,1,0:T(8,128)(2,1)}, u32[]{:S(2)}, u32[]{:S(2)}) async-start(bf16[8,1040,256]{2,1,0:T(8,128)(2,1)} %shard_map.64), calls=%async_computation | async-start | bytes 8519680 | tf_op jit(solution)/shard_map/all_to_all | solution.py:41
  12.8 6.0 %shard_map.65 = bf16[8,1536,256]{2,1,0:T(8,128)(2,1)} custom-call(bf16[256,8192]{1,0:T(8,128)(2,1)} %refs_0_.4, bf16[256,8192]{1,0:T(8,128)(2,1)} %refs_1_.3, bf16[256,8192]{1,0:T(8,128)(2,1)} %refs_0_.5), custom_call_target="tpu_custom_call" | custom-call | bytes 12582 | tf_op jit(solution)/shard_map/pallas_call | solution.py:113
  18.8 88.7 %all-to-all-done.k_ref.v_ref.rate_ref = bf16[8,1040,256]{2,1,0:T(8,128)(2,1)} async-done(((bf16[8,1040,256]{2,1,0:T(8,128)(2,1)}), bf16[8,1040,256]{2,1,0:T(8,128)(2,1)}, u32[]{:S(2)}, u32[]{:S(2)}) %all-to-all-start) | async-done | bytes 4259872 | tf_op jit(solution)/shard_map/all_to_all | solution.py:41
  107.5 4.8 %all-to-all-start.1 = ((bf16[8,1536,256]{2,1,0:T(8,128)(2,1)}), bf16[8,1536,256]{2,1,0:T(8,128)(2,1)}, u32[]{:S(2)}, u32[]{:S(2)}) async-start(bf16[8,1536,256]{2,1,0:T(8,128)(2,1)} %shard_map.65), calls=%async_computation.1 | async-start | bytes 12582912 | tf_op jit(solution)/shard_map/all_to_all | solution.py:41
  112.3 7.9 %shard_map.67 = f32[3,2,256,256]{3,2,1,0:T(8,128)} custom-call(bf16[8,1040,256]{2,1,0:T(8,128)(2,1)} %all-to-all-done.k_ref.v_ref.rate_ref, bf16[8,1040,256]{2,1,0:T(8,128)(2,1)} %all-to-all-done.k_ref.v_ref.rate_ref, bf16[8,1040,256]{2,1,0:T(8,128)(2,1)} %all-to-all-done.k_ref.v_ref.rate_ref, bf16[3,4,256,256]{3,2,1,0:T(8,128)(2,1)} %init_ref.3), custom_call_target="tpu_custom_call" | custom-call | flops 3221225 | bytes 4194 | tf_op jit(solution)/shard_map/pallas_call | solution.py:162
  121.7 3.1 collective-permute-done
  128.7 1.9 collective-permute-start.2
  130.6 2.7 shard_map.66
  133.3 22.1 %collective-permute-start.3 = (bf16[8,1040,256]{2,1,0:T(8,128)(2,1)}, bf16[8,1040,256]{2,1,0:T(8,128)(2,1)}, u32[]{:S(2)}, u32[]{:S(2)}) collective-permute-start(bf16[8,1040,256]{2,1,0:T(8,128)(2,1)} %all-to-all-done.k_ref.v_ref.rate_ref), channel_id=1, source_target_pairs={{0,8},{8,16},{16,24},{1,9},{9,17},{17,25},{2,10},{10,18},{18,26},{... | collective-permute-start | bytes 12779528 | tf_op jit(solution)/shard_map/ppermute | solution.py:37
  155.5 2.1 fusion.1
  157.6 2.8 multiply_convert_fusion.1.fit_ref
  160.4 89.2 %all-to-all-done.1.q_ref = bf16[8,1536,256]{2,1,0:T(8,128)(2,1)} async-done(((bf16[8,1536,256]{2,1,0:T(8,128)(2,1)}), bf16[8,1536,256]{2,1,0:T(8,128)(2,1)}, u32[]{:S(2)}, u32[]{:S(2)}) %all-to-all-start.1) | async-done | bytes 6291488 | tf_op jit(solution)/shard_map/all_to_all | solution.py:41
  249.6 4.3 %all-to-all-start.2 = ((bf16[8,512,256]{2,1,0:T(8,128)(2,1)}), bf16[8,512,256]{2,1,0:T(8,128)(2,1)}, u32[]{:S(2)}, u32[]{:S(2)}) async-start(bf16[8,512,256]{2,1,0:T(8,128)(2,1)} %shard_map.66), calls=%async_computation.2 | async-start | bytes 4194304 | tf_op jit(solution)/shard_map/all_to_all | solution.py:41
  253.9 4.5 %slice.10.k_ref.v_ref = bf16[8,1024,256]{2,1,0:T(8,128)(2,1)} slice(bf16[8,1536,256]{2,1,0:T(8,128)(2,1)} %all-to-all-done.1.q_ref), slice={[0:8], [0:1024], [0:256]} | slice | bytes 8388608 | tf_op jit(solution)/shard_map/slice | solution.py:345
  258.4 3.4 collective-permute-start.4
  261.7 7.9 %shard_map.68 = f32[3,2,256,256]{3,2,1,0:T(8,128)} custom-call(bf16[8,1024,256]{2,1,0:T(8,128)(2,1)} %slice.10.k_ref.v_ref, bf16[8,1024,256]{2,1,0:T(8,128)(2,1)} %slice.10.k_ref.v_ref, bf16[8,1040,256]{2,1,0:T(8,128)(2,1)} %all-to-all-done.k_ref.v_ref.rate_ref, bf16[3,4,256,256]{3,2,1,0:T(8,128)(2,1)} %init_ref.3), custom_call_target="tpu_custom_call" | custom-call | flops 3221225 | bytes 4194 | tf_op jit(solution)/shard_map/pallas_call | solution.py:162
  271.1 2.3 collective-permute-start.5
  274.0 21.0 %shard_map.69 = bf16[8,2,256,256]{3,2,1,0:T(8,128)(2,1)} custom-call(s32[2]{0:T(128)} %pad_add_fusion.place_ref, bf16[8,1536,256]{2,1,0:T(8,128)(2,1)} %all-to-all-done.1.q_ref, bf16[8,1040,256]{2,1,0:T(8,128)(2,1)} %all-to-all-done.k_ref.v_ref.rate_ref, bf16[8,1040,256]{2,1,0:T(8,128)(2,1)} %all-to-all-done.k_ref.v_ref.rate_ref, ...), custom_call_target="tpu_custom_call" | custom-call | flops 11274289 | bytes 12582 | tf_op jit(solution)/shard_map/pallas_call | solution.py:229
  295.0 6.6 %all-to-all-done.2.q_ref = bf16[8,512,256]{2,1,0:T(8,128)(2,1)} async-done(((bf16[8,512,256]{2,1,0:T(8,128)(2,1)}), bf16[8,512,256]{2,1,0:T(8,128)(2,1)}, u32[]{:S(2)}, u32[]{:S(2)}) %all-to-all-start.2) | async-done | bytes 2097184 | tf_op jit(solution)/shard_map/all_to_all | solution.py:41
  301.7 4.3 %all-to-all-start.3 = ((bf16[8,2,256,256]{3,2,1,0:T(8,128)(2,1)}), bf16[8,2,256,256]{3,2,1,0:T(8,128)(2,1)}, u32[]{:S(2)}, u32[]{:S(2)}) async-start(bf16[8,2,256,256]{3,2,1,0:T(8,128)(2,1)} %shard_map.69), calls=%async_computation.3 | async-start | bytes 4194304 | tf_op jit(solution)/shard_map/all_to_all | solution.py:41
  310.4 21.1 %shard_map.70 = (bf16[2,256,256]{2,1,0:T(8,128)(2,1)}, bf16[2,256,256]{2,1,0:T(8,128)(2,1)}, bf16[2,256,256]{2,1,0:T(8,128)(2,1)}, bf16[2,256,256]{2,1,0:T(8,128...) custom-call(s32[2]{0:T(128)} %pad_add_fusion.place_ref, ...), custom_call_target="tpu_custom_call" | custom-call | flops 11274289 | bytes 12582 | tf_op jit(solution)/shard_map/pallas_call | solution.py:229
  331.5 2.0 collective-permute-start.8
  334.9 3.3 collective-permute-start.10
  340.3 2.6 collective-permute-done.8.refs_0_
  342.9 4.0 collective-permute-start.13
  346.9 2.1 collective-permute-start.14
  348.9 8.5 %collective-permute-done.10.refs_2_ = bf16[2,256,256]{2,1,0:T(8,128)(2,1)S(1)} collective-permute-done((bf16[2,256,256]{2,1,0:T(8,128)(2,1)}, bf16[2,256,256]{2,1,0:T(8,128)(2,1)S(1)}, u32[]{:S(2)}, u32[]{:S(2)}) %collective-permute-start.10) | collective-permute-done | bytes 262176 | tf_op jit(solution)/shard_map/ppermute | solution.py:265
  357.5 3.7 collective-permute-done.11.refs_3_
  361.2 35.3 %collective-permute-done.12.refs_4_ = bf16[2,256,256]{2,1,0:T(8,128)(2,1)S(1)} collective-permute-done((bf16[2,256,256]{2,1,0:T(8,128)(2,1)}, bf16[2,256,256]{2,1,0:T(8,128)(2,1)S(1)}, u32[]{:S(2)}, u32[]{:S(2)}) %collective-permute-start.12) | collective-permute-done | bytes 262176 | tf_op jit(solution)/shard_map/ppermute | solution.py:265
  396.5 2.3 collective-permute-done.13.refs_5_
  399.6 4.6 %shard_map.71 = bf16[256,8192]{1,0:T(8,128)(2,1)} custom-call(s32[2]{0:T(128)} %pad_add_fusion.place_ref, bf16[8,2,256,256]{3,2,1,0:T(8,128)(2,1)} %all-to-all-done.3.first_ref, bf16[2,256,256]{2,1,0:T(8,128)(2,1)} %copy-done.4, bf16[2,256,256]{2,1,0:T(8,128)(2,1)} %copy-done.5, bf16[2,256,256]{2,1,0:T(8,128)(2,1)} %copy-done.6, ...), custom_call_target="tpu_custom_call" | custom-call | flops 10485 | bytes 8388 | tf_op jit(solution)/shard_map/pallas_call | solution.py:295
  (50 shorter events, 16.0 us)
Async XLA Ops:
  5.5 102.0 %all-to-all-start = ((bf16[8,1040,256]{2,1,0:T(8,128)(2,1)}), bf16[8,1040,256]{2,1,0:T(8,128)(2,1)}, u32[]{:S(2)}, u32[]{:S(2)}) async-start(bf16[8,1040,256]{2,1,0:T(8,128)(2,1)} %shard_map.64), calls=%async_computation | async-start | bytes 8519680 | tf_op jit(solution)/shard_map/all_to_all | solution.py:41
  107.5 142.0 %all-to-all-start.1 = ((bf16[8,1536,256]{2,1,0:T(8,128)(2,1)}), bf16[8,1536,256]{2,1,0:T(8,128)(2,1)}, u32[]{:S(2)}, u32[]{:S(2)}) async-start(bf16[8,1536,256]{2,1,0:T(8,128)(2,1)} %shard_map.65), calls=%async_computation.1 | async-start | bytes 12582912 | tf_op jit(solution)/shard_map/all_to_all | solution.py:41
  120.2 7.0 %copy-start.3 = (f32[3,2,256,256]{3,2,1,0:T(8,128)S(1)}, f32[3,2,256,256]{3,2,1,0:T(8,128)}, u32[]{:S(2)}) copy-start(f32[3,2,256,256]{3,2,1,0:T(8,128)} %shard_map.67) | copy-start | bytes 4718596
  120.2 4.6 %collective-permute-start = (f32[3,2,256,256]{3,2,1,0:T(8,128)}, f32[3,2,256,256]{3,2,1,0:T(8,128)S(1)}, u32[]{:S(2)}, u32[]{:S(2)}) collective-permute-start(f32[3,2,256,256]{3,2,1,0:T(8,128)} %shard_map.67), channel_id=1, source_target_pairs={{0,8},{1,9},{2,10},{3,11},{4,12},{5,13},{6,14},{7,15}} | collective-permute-start | bytes 4718600 | tf_op jit(solution)/shard_map/ppermute | solution.py:315
  126.4 0.8 collective-permute-start.1
  128.7 26.8 %copy-start = (bf16[3,4,256,256]{3,2,1,0:T(8,128)(2,1)S(1)}, bf16[3,4,256,256]{3,2,1,0:T(8,128)(2,1)}, u32[]{:S(2)}) copy-start(bf16[3,4,256,256]{3,2,1,0:T(8,128)(2,1)} %init_ref.3) | copy-start | bytes 4718596
  128.7 26.8 %collective-permute-start.2 = (f32[3,2,256,256]{3,2,1,0:T(8,128)}, f32[3,2,256,256]{3,2,1,0:T(8,128)}, u32[]{:S(2)}, u32[]{:S(2)}) collective-permute-start(f32[3,2,256,256]{3,2,1,0:T(8,128)} %get-tuple-element.38), channel_id=1, source_target_pairs={{16,24},{17,25},{18,26},{19,27},{20,28},{21,29},{22,30},{23,31}} | collective-permute-start | bytes 4718600 | tf_op jit(solution)/shard_map/ppermute | solution.py:315
  133.3 140.7 %collective-permute-start.3 = (bf16[8,1040,256]{2,1,0:T(8,128)(2,1)}, bf16[8,1040,256]{2,1,0:T(8,128)(2,1)}, u32[]{:S(2)}, u32[]{:S(2)}) collective-permute-start(bf16[8,1040,256]{2,1,0:T(8,128)(2,1)} %all-to-all-done.k_ref.v_ref.rate_ref), channel_id=1, source_target_pairs={{0,8},{8,16},{16,24},{1,9},{9,17},{17,25},{2,10},{10,18},{18,26},{... | collective-permute-start | bytes 12779528 | tf_op jit(solution)/shard_map/ppermute | solution.py:37
  249.6 52.1 %all-to-all-start.2 = ((bf16[8,512,256]{2,1,0:T(8,128)(2,1)}), bf16[8,512,256]{2,1,0:T(8,128)(2,1)}, u32[]{:S(2)}, u32[]{:S(2)}) async-start(bf16[8,512,256]{2,1,0:T(8,128)(2,1)} %shard_map.66), calls=%async_computation.2 | async-start | bytes 4194304 | tf_op jit(solution)/shard_map/all_to_all | solution.py:41
  258.4 52.0 %collective-permute-start.4 = (bf16[8,1024,256]{2,1,0:T(8,128)(2,1)}, bf16[8,1024,256]{2,1,0:T(8,128)(2,1)}, u32[]{:S(2)}, u32[]{:S(2)}) collective-permute-start(bf16[8,1024,256]{2,1,0:T(8,128)(2,1)} %slice.10.k_ref.v_ref), channel_id=1, source_target_pairs={{0,8},{8,16},{16,24},{1,9},{9,17},{17,25},{2,10},{10,18},{18,26},{... | collective-permute-start | bytes 12582920 | tf_op jit(solution)/shard_map/ppermute | solution.py:37
  271.1 34.9 %collective-permute-start.5 = (bf16[3,2,256,256]{3,2,1,0:T(8,128)(2,1)S(1)}, bf16[3,2,256,256]{3,2,1,0:T(8,128)(2,1)S(1)}, u32[]{:S(2)}, u32[]{:S(2)}) collective-permute-start(bf16[3,2,256,256]{3,2,1,0:T(8,128)(2,1)S(1)} %convert_element_type.33), channel_id=1, source_target_pairs={{0,8},{1,9},{2,10},{3,11},{4,12},{5,13},{6,14},{7,15}} | collective-permute-start | bytes 2359304 | tf_op jit(solution)/shard_map/ppermute | solution.py:315
  295.0 11.0 %copy-start.2 = (f32[3,2,256,256]{3,2,1,0:T(8,128)S(1)}, f32[3,2,256,256]{3,2,1,0:T(8,128)}, u32[]{:S(2)}) copy-start(f32[3,2,256,256]{3,2,1,0:T(8,128)} %shard_map.68) | copy-start | bytes 4718596
  301.7 97.1 %all-to-all-start.3 = ((bf16[8,2,256,256]{3,2,1,0:T(8,128)(2,1)}), bf16[8,2,256,256]{3,2,1,0:T(8,128)(2,1)}, u32[]{:S(2)}, u32[]{:S(2)}) async-start(bf16[8,2,256,256]{3,2,1,0:T(8,128)(2,1)} %shard_map.69), calls=%async_computation.3 | async-start | bytes 4194304 | tf_op jit(solution)/shard_map/all_to_all | solution.py:41
  306.2 2.2 copy-start.1
  306.3 0.9 collective-permute-start.6
  307.4 1.0 collective-permute-start.7
  331.5 11.4 %collective-permute-start.8 = (bf16[2,256,256]{2,1,0:T(8,128)(2,1)}, bf16[2,256,256]{2,1,0:T(8,128)(2,1)S(1)}, u32[]{:S(2)}, u32[]{:S(2)}) collective-permute-start(bf16[2,256,256]{2,1,0:T(8,128)(2,1)} %get-tuple-element.27), channel_id=1, source_target_pairs={{0,2},{1,3},{2,0},{3,1},{4,6},{5,7},{6,4},{7,5},{8,10},{9,11},{10,... | collective-permute-start | bytes 786440 | tf_op jit(solution)/shard_map/ppermute | solution.py:265
  333.5 13.4 %collective-permute-start.9 = (bf16[2,256,256]{2,1,0:T(8,128)(2,1)}, bf16[2,256,256]{2,1,0:T(8,128)(2,1)S(1)}, u32[]{:S(2)}, u32[]{:S(2)}) collective-permute-start(bf16[2,256,256]{2,1,0:T(8,128)(2,1)} %get-tuple-element.28), channel_id=1, source_target_pairs={{0,3},{1,2},{2,1},{3,0},{4,7},{5,6},{6,5},{7,4},{8,11},{9,10},{10,... | collective-permute-start | bytes 786440 | tf_op jit(solution)/shard_map/ppermute | solution.py:265
  334.9 22.5 %collective-permute-start.10 = (bf16[2,256,256]{2,1,0:T(8,128)(2,1)}, bf16[2,256,256]{2,1,0:T(8,128)(2,1)S(1)}, u32[]{:S(2)}, u32[]{:S(2)}) collective-permute-start(bf16[2,256,256]{2,1,0:T(8,128)(2,1)} %get-tuple-element.29), channel_id=1, source_target_pairs={{0,7},{1,6},{2,5},{3,4},{4,3},{5,2},{6,1},{7,0},{8,15},{9,14},{10,... | collective-permute-start | bytes 786440 | tf_op jit(solution)/shard_map/ppermute | solution.py:265
  338.2 23.0 %collective-permute-start.11 = (bf16[2,256,256]{2,1,0:T(8,128)(2,1)}, bf16[2,256,256]{2,1,0:T(8,128)(2,1)S(1)}, u32[]{:S(2)}, u32[]{:S(2)}) collective-permute-start(bf16[2,256,256]{2,1,0:T(8,128)(2,1)} %get-tuple-element.30), channel_id=1, source_target_pairs={{0,6},{1,7},{2,4},{3,5},{4,2},{5,3},{6,0},{7,1},{8,14},{9,15},{10,... | collective-permute-start | bytes 786440 | tf_op jit(solution)/shard_map/ppermute | solution.py:265
  338.3 58.1 %collective-permute-start.12 = (bf16[2,256,256]{2,1,0:T(8,128)(2,1)}, bf16[2,256,256]{2,1,0:T(8,128)(2,1)S(1)}, u32[]{:S(2)}, u32[]{:S(2)}) collective-permute-start(bf16[2,256,256]{2,1,0:T(8,128)(2,1)} %get-tuple-element.31), channel_id=1, source_target_pairs={{0,5},{1,4},{2,7},{3,6},{4,1},{5,0},{6,3},{7,2},{8,13},{9,12},{10,... | collective-permute-start | bytes 786440 | tf_op jit(solution)/shard_map/ppermute | solution.py:265
  342.9 55.9 %copy-start.4 = (bf16[2,256,256]{2,1,0:T(8,128)(2,1)}, bf16[2,256,256]{2,1,0:T(8,128)(2,1)S(1)}, u32[]{:S(2)}) copy-start(bf16[2,256,256]{2,1,0:T(8,128)(2,1)S(1)} %collective-permute-done.8.refs_0_) | copy-start | bytes 786436
  342.9 55.9 %collective-permute-start.13 = (bf16[2,256,256]{2,1,0:T(8,128)(2,1)}, bf16[2,256,256]{2,1,0:T(8,128)(2,1)S(1)}, u32[]{:S(2)}, u32[]{:S(2)}) collective-permute-start(bf16[2,256,256]{2,1,0:T(8,128)(2,1)} %get-tuple-element.32), channel_id=1, source_target_pairs={{0,4},{1,5},{2,6},{3,7},{4,0},{5,1},{6,2},{7,3},{8,12},{9,13},{10,... | collective-permute-start | bytes 786440 | tf_op jit(solution)/shard_map/ppermute | solution.py:265
  346.9 51.9 %copy-start.5 = (bf16[2,256,256]{2,1,0:T(8,128)(2,1)}, bf16[2,256,256]{2,1,0:T(8,128)(2,1)S(1)}, u32[]{:S(2)}) copy-start(bf16[2,256,256]{2,1,0:T(8,128)(2,1)S(1)} %collective-permute-done.9.refs_1_) | copy-start | bytes 786436
  346.9 51.9 %collective-permute-start.14 = (bf16[2,256,256]{2,1,0:T(8,128)(2,1)}, bf16[2,256,256]{2,1,0:T(8,128)(2,1)S(1)}, u32[]{:S(2)}, u32[]{:S(2)}) collective-permute-start(bf16[2,256,256]{2,1,0:T(8,128)(2,1)} %get-tuple-element.33), channel_id=1, source_target_pairs={{0,1},{1,0},{2,3},{3,2},{4,5},{5,4},{6,7},{7,6},{8,9},{9,8},{10,11... | collective-permute-start | bytes 786440 | tf_op jit(solution)/shard_map/ppermute | solution.py:265
  357.5 41.3 %copy-start.6 = (bf16[2,256,256]{2,1,0:T(8,128)(2,1)}, bf16[2,256,256]{2,1,0:T(8,128)(2,1)S(1)}, u32[]{:S(2)}) copy-start(bf16[2,256,256]{2,1,0:T(8,128)(2,1)S(1)} %collective-permute-done.10.refs_2_) | copy-start | bytes 786436
  361.2 37.6 %copy-start.7 = (bf16[2,256,256]{2,1,0:T(8,128)(2,1)}, bf16[2,256,256]{2,1,0:T(8,128)(2,1)S(1)}, u32[]{:S(2)}) copy-start(bf16[2,256,256]{2,1,0:T(8,128)(2,1)S(1)} %collective-permute-done.11.refs_3_) | copy-start | bytes 786436
  396.5 2.4 copy-start.8
  398.8 0.7 copy-start.9
  398.8 0.8 copy-start.10
